TPU v7x, 32 devices: a whole 2x2x4 slice. The times are simulated.
32 devices in a mesh: row: 8 (over y, x, core), col: 4 (over z).
Axes of the slice: x: 2, y: 2, z: 4, core: 2. Of those that a mesh axis runs over, the one named last changes fastest.
Arguments:
- video_rows: bfloat16 [12288, 1024], P(('row', 'col')), may hold values from -1.5 to 1.5
- video_ids: int32 [12288], P(('row', 'col')), may hold values from 0 to 767
- imu_rows: bfloat16 [12288, 1024], P(('row', 'col')), may hold values from -1.5 to 1.5
- imu_ids: int32 [12288], P(('row', 'col')), may hold values from 0 to 767
- audio_rows: bfloat16 [12288, 1024], P(('row', 'col')), may hold values from -1.5 to 1.5
- audio_ids: int32 [12288], P(('row', 'col')), may hold values from 0 to 767
- imu_log_scale: float32 [1], replicated, may hold values from 0 to 1
- imu_bias: float32 [1], replicated, may hold values from -3 to -1
- audio_log_scale: float32 [1], replicated, may hold values from 0 to 1
- audio_bias: float32 [1], replicated, may hold values from -3 to -1
Outputs:
- video_grad: float32 [12288, 1024], P(('row', 'col'))
- imu_grad: float32 [12288, 1024], P(('row', 'col'))
- audio_grad: float32 [12288, 1024], P(('row', 'col'))
- row_loss: float32 [12288], P(('row', 'col'))
All inputs are finite; a program needn't handle non-finite values.
Results may differ from a plain program's by a relative error of at most 0.0025.
Values may be sent and summed in bfloat16 or wider, within the bound.
No kernel may reach another device: no remote copies, remote signals or barrier semaphores. Data moves between devices by JAX's collectives and lax.ppermute only.
A program may use at most 128 MiB of HBM per device.

v0:
```python
import jax
import jax.numpy as jnp
from jax import lax
from jax.experimental import pallas as pl
from jax.experimental.pallas import tpu as pltpu
from jax.sharding import PartitionSpec as P

STEPS = 4
SLAB = 16
COLUMNS = 512
SUM_BLOCKS = 4
TAG_ROWS = 16
TAG_BASE = 256
COSTS = {
    "own": 0.5e9, "col_own": 0.5e9, "row": 0.5e9, "col_far": 0.5e9,
    "col_near": 0.5e9, "row_sum": 0.5e9, "audio_sum": 5e9, "video_sum": 20e9,
}

F32 = jnp.float32
BF16 = jnp.bfloat16


def pack_kernel(*refs):
    blocks, ids, packed = refs[:2], refs[2:4], refs[4:6]
    tags, (block_done, tags_done) = refs[6:8], refs[8:]
    rows, width = blocks[0].shape
    copies = [
        pltpu.make_async_copy(block, out.at[:rows, :], block_done.at[k])
        for k, (block, out) in enumerate(zip(blocks, packed))
    ]
    tag_copies = [
        pltpu.make_async_copy(source, tags[k], tags_done.at[k]) for k, source in enumerate(ids)
    ]
    for copy in tag_copies + copies:
        copy.start()
    for copy in tag_copies:
        copy.wait()
    for k, out in enumerate(packed):
        tag = tags[k][...].reshape(1, rows)
        high = tag // TAG_BASE
        low = tag - high * TAG_BASE
        both = jnp.concatenate([high, low, jnp.zeros((TAG_ROWS - 2, rows), jnp.int32)], axis=0)
        out[rows:, :rows] = both.astype(F32).astype(BF16)
        out[rows:, rows:] = jnp.zeros((TAG_ROWS, width - rows), BF16)
    for copy in copies:
        copy.wait()


def pack(blocks, ids):
    rows, width = blocks[0].shape
    hbm, vmem = pl.BlockSpec(memory_space=pltpu.HBM), pl.BlockSpec(memory_space=pltpu.VMEM)
    return pl.pallas_call(
        pack_kernel,
        out_shape=[pltpu.VMEM((rows + TAG_ROWS, width), BF16)] * 2,
        in_specs=[hbm] * 4,
        out_specs=[vmem] * 2,
        scratch_shapes=[
            *[pltpu.VMEM((rows,), jnp.int32)] * 2,
            pltpu.SemaphoreType.DMA((2,)),
            pltpu.SemaphoreType.DMA((2,)),
        ],
        compiler_params=pltpu.CompilerParams(vmem_limit_bytes=56 * 2**20),
    )(*blocks, *ids)


def tags_of(block):
    if isinstance(block, tuple):
        tags = block[1][...]
        return tags.reshape(1, tags.shape[0]).astype(F32)
    rows = block.shape[0] - TAG_ROWS
    tags = block[rows:, :rows].astype(F32)
    return tags[0:1] * TAG_BASE + tags[1:2]


def rows_of(block):
    return block[0] if isinstance(block, tuple) else block


def meet(video, partner, scalars, products, weights):
    rows = weights.shape[0]
    log_scale, offset = scalars[0][0], scalars[1][0]
    scale = jnp.exp(jnp.full((1, rows), log_scale, F32))
    products[...] = lax.dot_general(
        rows_of(partner)[:rows, :], video[:rows, :], (((1,), (1,)), ((), ())), preferred_element_type=F32
    )
    video_tags = tags_of(video)
    partner_tags = jnp.transpose(jnp.broadcast_to(tags_of(partner), (8, rows)))[:, :1]
    total = jnp.zeros((8, rows), F32)
    for start in range(0, rows, SLAB):
        part = slice(start, start + SLAB)
        logits = scale * products[part, :] + offset
        same = partner_tags[part, :] == video_tags
        flipped = -logits
        z = jnp.where(same, flipped, logits)
        e = jnp.exp(jnp.minimum(logits, flipped))
        inverse = 1.0 / (1.0 + e)
        sigmoid = jnp.where(z >= 0.0, inverse, e * inverse)
        weights[part, :] = (jnp.where(same, -scale, scale) * sigmoid).astype(BF16)
        log1p = jnp.where(e < 0.005, e * (1.0 - 0.5 * e), jnp.log(1.0 + e))
        losses = jnp.maximum(z, 0.0) + log1p
        total = total + jnp.sum(losses.reshape(SLAB // 8, 8, rows), axis=0)
    return jnp.sum(total, axis=0, keepdims=True)


def column_parts(ref):
    return [slice(c, c + COLUMNS) for c in range(0, ref.shape[1], COLUMNS)]


def to_video(weights, partner, part):
    rows = weights.shape[0]
    return lax.dot_general(
        weights[...], rows_of(partner)[:rows, part], (((0,), (0,)), ((), ())), preferred_element_type=F32
    )


def to_partner(weights, video, part):
    return jnp.dot(weights[...], video[: weights.shape[0], part], preferred_element_type=F32)


def own_kernel(
    imu_log_scale, imu_bias, audio_log_scale, audio_bias, video, imu, audio, audio_ids,
    loss, video_grad, imu_grad, audio_grad, video_on, imu_on, products, weights,
):
    video_on[...] = video[...]
    imu_on[...] = imu[...]
    audio = (audio, audio_ids)
    loss[...] = meet(video, audio, (audio_log_scale, audio_bias), products, weights)
    for part in column_parts(video):
        video_grad[:, part] = to_video(weights, audio, part)
        audio_grad[:, part] = to_partner(weights, video, part)
    loss[...] += meet(video, imu, (imu_log_scale, imu_bias), products, weights)
    for part in column_parts(video):
        video_grad[:, part] += to_video(weights, imu, part)
        imu_grad[:, part] = to_partner(weights, video, part)


def put_losses(losses, packed):
    rows = losses.shape[1]
    terms = []
    for _ in range(3):
        terms.append(losses.astype(BF16).astype(F32))
        losses = losses - terms[-1]
    terms.append(jnp.zeros((TAG_ROWS - 3, rows), F32))
    packed[rows:, :rows] = jnp.concatenate(terms, axis=0).astype(BF16)
    packed[rows:, rows:] = jnp.zeros((TAG_ROWS, packed.shape[1] - rows), BF16)


def row_kernel(
    log_scale, bias, video, other_video, imu, other_imu, loss_in, video_in, grad_in,
    loss, video_grad, grad, other_grad, sums, products, weights, other_weights, near_weights,
):
    scalars = (log_scale, bias)
    rows = sums.shape[0]
    losses = meet(other_video, imu, scalars, products, near_weights)
    losses = losses + meet(other_video, other_imu, scalars, products, other_weights)
    put_losses(losses, other_grad)
    loss[...] = loss_in[...] + meet(video, other_imu, scalars, products, weights)
    for part in column_parts(video):
        other_sum = to_video(near_weights, imu, part) + to_video(other_weights, other_imu, part)
        other_grad[:rows, part] = other_sum.astype(BF16)
        both = to_partner(weights, video, part) + to_partner(other_weights, other_video, part)
        sums[:, part] = both.astype(BF16)
        grad[:, part] = grad_in[:, part] + to_partner(near_weights, other_video, part)
        video_grad[:, part] = video_in[:, part] + to_video(weights, other_imu, part)


def col_own_kernel(
    log_scale, bias, video, audio, audio_ids, loss_in, video_in,
    loss, video_grad, sums, products, weights,
):
    audio = (audio, audio_ids)
    loss[...] = loss_in[...] + meet(video, audio, (log_scale, bias), products, weights)
    for part in column_parts(video):
        video_grad[:, part] = video_in[:, part] + to_video(weights, audio, part)
        sums[:, part] = to_partner(weights, video, part)


def col_far_kernel(
    log_scale, bias, other_video, audio, audio_ids, sums_in, loss_in,
    other_loss, other_grad, sums, loss, products, weights,
):
    loss[...] = loss_in[...]
    audio = (audio, audio_ids)
    other_loss[...] = meet(other_video, audio, (log_scale, bias), products, weights)
    for part in column_parts(other_video):
        sums[:, part] = (sums_in[:, part] + to_partner(weights, other_video, part)).astype(BF16)
        other_grad[:, part] = to_video(weights, audio, part)


def col_near_kernel(
    log_scale, bias, other_video, audio, audio_ids, other_loss_in, other_in, grad_in, loss_in,
    other_grad, grad, loss, products, weights,
):
    loss[...] = loss_in[...]
    audio = (audio, audio_ids)
    rows = grad.shape[0]
    losses = meet(other_video, audio, (log_scale, bias), products, weights)
    put_losses(other_loss_in[...] + losses, other_grad)
    for part in column_parts(other_video):
        other_sum = other_in[:, part] + to_video(weights, audio, part)
        other_grad[:rows, part] = other_sum.astype(BF16)
        grad[:, part] = grad_in[:, part] + to_partner(weights, other_video, part)


def added(parts, out, buffer, done):
    rows = out.shape[0] // SUM_BLOCKS
    copies = []
    for k in range(SUM_BLOCKS):
        block = slice(k * rows, (k + 1) * rows)
        total = parts[0][block, :]
        for part in parts[1:]:
            total = total + part[block, :].astype(F32)
        buffer[block, :] = total
        copy = pltpu.make_async_copy(buffer.at[block, :], out.at[block, :], done.at[k])
        copy.start()
        copies.append(copy)
    return copies


def losses_in(packed):
    rows = packed.shape[0] - TAG_ROWS
    return jnp.sum(packed[rows:, :rows].astype(F32), axis=0, keepdims=True)


def audio_sum_kernel(got_audio, audio_in, loss_in, audio_grad, loss, buffer, done):
    copies = added((audio_in, got_audio), audio_grad, buffer, done)
    loss[...] = loss_in[...]
    for copy in copies:
        copy.wait()


def video_sum_kernel(got_video, video_in, loss_in, video_grad, loss):
    rows = video_grad.shape[0]
    video_grad[...] = video_in[...] + got_video[:rows, :].astype(F32)
    loss[...] = loss_in[...] + losses_in(got_video)


def row_sum_kernel(
    got_video, got_imu, video_in, imu_in, loss_in, video_grad, imu_grad, loss,
    video_buffer, video_done, imu_buffer, imu_done,
):
    copies = added((video_in, got_video), video_grad, video_buffer, video_done)
    copies += added((imu_in, got_imu), imu_grad, imu_buffer, imu_done)
    rows = video_in.shape[0]
    total = loss_in[...] + losses_in(got_video)
    loss[...] = (total / (2.0 * STEPS * rows)).reshape(rows)
    for copy in copies:
        copy.wait()


def summed(kernel, outs, spaces, args, cost):
    vmem = pl.BlockSpec(memory_space=pltpu.VMEM)
    return pl.pallas_call(
        kernel,
        out_shape=[jax.ShapeDtypeStruct(*out) for out in outs],
        in_specs=[vmem] * len(args),
        out_specs=[pl.BlockSpec(memory_space=space) for space in spaces],
        scratch_shapes=[pltpu.VMEM(outs[0][0], F32), pltpu.SemaphoreType.DMA((SUM_BLOCKS,))]
        * sum(space == pltpu.HBM for space in spaces),
        compiler_params=pltpu.CompilerParams(vmem_limit_bytes=20 * 2**20),
        cost_estimate=pl.CostEstimate(flops=int(cost), bytes_accessed=0, transcendentals=0),
    )(*args)


def call(kernel, outs, scalars, args, rows, weights=1, cost=0):
    smem, vmem = pl.BlockSpec(memory_space=pltpu.SMEM), pl.BlockSpec(memory_space=pltpu.VMEM)
    scratch = [pltpu.VMEM((rows, rows), F32)] + [pltpu.VMEM((rows, rows), BF16)] * weights
    return pl.pallas_call(
        kernel,
        out_shape=[jax.ShapeDtypeStruct(*out) for out in outs],
        in_specs=[smem] * len(scalars) + [vmem] * len(args),
        out_specs=[vmem] * len(outs),
        scratch_shapes=scratch,
        compiler_params=pltpu.CompilerParams(vmem_limit_bytes=20 * 2**20),
        cost_estimate=pl.CostEstimate(
            flops=int(cost),
            bytes_accessed=2 * sum(a.size * a.dtype.itemsize for a in args),
            transcendentals=0,
        ),
    )(*scalars, *args)


class Tile:
    def __init__(self, axis):
        self.axis = axis
        devices = lax.axis_size(axis)
        if devices == STEPS:
            self.video = [(p ^ 1, p) for p in range(devices)]
            self.partner = [(p ^ 2, p) for p in range(devices)]
        else:
            self.video = [((p + 1) % devices, p) for p in range(devices)]
            self.partner = [((p - 2) % devices, p) for p in range(devices)]

    def bring_video(self, block):
        return lax.ppermute(block, self.axis, self.video)

    def bring_partner(self, block):
        return lax.ppermute(block, self.axis, self.partner)

    def return_video(self, block):
        return lax.ppermute(block, self.axis, [(b, a) for a, b in self.video])

    def return_partner(self, block):
        return lax.ppermute(block, self.axis, [(b, a) for a, b in self.partner])


def per_device(
    video, video_ids, imu, imu_ids, audio, audio_ids,
    imu_log_scale, imu_bias, audio_log_scale, audio_bias,
):
    rows, width = video.shape
    line, square, narrow = ((1, rows), F32), ((rows, width), F32), ((rows, width), BF16)
    packed = ((rows + TAG_ROWS, width), BF16)
    of_imu, of_audio = (imu_log_scale, imu_bias), (audio_log_scale, audio_bias)
    along_row, along_col = Tile("row"), Tile("col")

    col_audio = along_col.bring_partner(audio), along_col.bring_partner(audio_ids)
    audio = (audio, audio_ids)
    video, imu = pack((video, imu), (video_ids, imu_ids))
    col_video = along_col.bring_video(video)

    loss, video_grad, imu_grad, audio_grad, video_on, imu_on = call(
        own_kernel,
        [line, square, square, square, packed, packed],
        of_imu + of_audio,
        (video, imu, *audio),
        rows, 1, COSTS["own"],
    )
    row_video = along_row.bring_video(video_on)
    row_imu = along_row.bring_partner(imu_on)
    loss, video_grad, sums = call(
        col_own_kernel,
        [line, square, square],
        of_audio,
        (video, *col_audio, loss, video_grad),
        rows, 1, COSTS["col_own"],
    )
    col_loss, col_grad, sums, loss = call(
        col_far_kernel,
        [line, square, narrow, line],
        of_audio,
        (col_video, *col_audio, sums, loss),
        rows, 1, COSTS["col_far"],
    )
    got_audio = along_col.return_partner(sums)
    col_grad, audio_grad, loss = call(
        col_near_kernel,
        [packed, square, line],
        of_audio,
        (col_video, *audio, col_loss, col_grad, audio_grad, loss),
        rows, 1, COSTS["col_near"],
    )
    got_col = along_col.return_video(col_grad)

    loss, video_grad, imu_grad, row_grad, row_sums = call(
        row_kernel,
        [line, square, square, packed, narrow],
        of_imu,
        (video, row_video, imu, row_imu, loss, video_grad, imu_grad),
        rows, 3, COSTS["row"],
    )
    got_row = along_row.return_video(row_grad)
    got_imu = along_row.return_partner(row_sums)

    hbm, vmem = pltpu.HBM, pltpu.VMEM
    audio_grad, loss = summed(
        audio_sum_kernel,
        [square, line],
        [hbm, vmem],
        (got_audio, audio_grad, loss),
        COSTS["audio_sum"],
    )
    video_grad, loss = summed(
        video_sum_kernel,
        [square, line],
        [vmem, vmem],
        (got_col, video_grad, loss),
        COSTS["video_sum"],
    )
    video_grad, imu_grad, loss = summed(
        row_sum_kernel,
        [square, square, ((rows,), F32)],
        [hbm, hbm, vmem],
        (got_row, got_imu, video_grad, imu_grad, loss),
        COSTS["row_sum"],
    )
    return (video_grad, imu_grad, audio_grad, loss)


def solution(mesh):
    rows, vector = P(("row", "col"), None), P(("row", "col"))
    return jax.shard_map(
        per_device,
        mesh=mesh,
        in_specs=(rows, vector, rows, vector, rows, vector, P(), P(), P(), P()),
        out_specs=(rows, rows, rows, vector),
        check_vma=False,
    )
```

profile of v0, /device:TPU:0, one launch (start us, length us, event | category | flops | bytes accessed | tf_op | source)
XLA Modules:
  0.0 86.1 jit_solution(10663361576179227952)
XLA Ops:
  0.6 0.0 copy-start
  0.6 0.0 copy-start.1
  0.7 4.1 %collective-permute-start.3 = (bf16[384,1024]{1,0:T(8,128)(2,1)}, bf16[384,1024]{1,0:T(8,128)(2,1)S(1)}, u32[]{:S(2)}, u32[]{:S(2)}) collective-permute-start(bf16[384,1024]{1,0:T(8,128)(2,1)} %audio.3), channel_id=1, source_target_pairs={{2,0},{3,1},{0,2},{1,3},{6,4},{7,5},{4,6},{5,7},{10,8},{11,9},{8,1... | collective-permute-start | bytes 2359304 | tf_op jit(solution)/shard_map/ppermute | solution.py:298
  4.8 1.4 %shard_map.129 = (bf16[400,1024]{1,0:T(8,128)(2,1)S(1)}, bf16[400,1024]{1,0:T(8,128)(2,1)S(1)}) custom-call(bf16[384,1024]{1,0:T(8,128)(2,1)} %refs_0_.1, bf16[384,1024]{1,0:T(8,128)(2,1)} %refs_1_.1, s32[384]{0:T(512)} %refs_2_.1, s32[384]{0:T(512)} %refs_3_.1), custom_call_target="tpu_custom_call" | custom-call | tf_op jit(solution)/shard_map/pallas_call | solution.py:52
  6.2 1.6 %collective-permute-start.2 = (bf16[400,1024]{1,0:T(8,128)(2,1)S(1)}, bf16[400,1024]{1,0:T(8,128)(2,1)S(1)}, u32[]{:S(2)}, u32[]{:S(2)}) collective-permute-start(bf16[400,1024]{1,0:T(8,128)(2,1)S(1)} %get-tuple-element.34.video), channel_id=1, source_target_pairs={{1,0},{0,1},{3,2},{2,3},{5,4},{4,5},{7,6},{6,7},{9,8},{8,9},{11,10... | collective-permute-start | bytes 2457608 | tf_op jit(solution)/shard_map/ppermute | solution.py:295
  7.8 0.0 copy-done.1
  7.8 0.3 collective-permute-start.4
  10.8 0.0 copy-done
  10.8 3.8 %shard_map.130 = (f32[1,384]{1,0:T(1,128)S(1)}, f32[384,1024]{1,0:T(8,128)S(1)}, f32[384,1024]{1,0:T(8,128)S(1)}, f32[384,1024]{1,0:T(8,128)S(1)}, bf16[400,1024...) custom-call(f32[1]{0:T(128)S(6)} %copy.14.imu_log_scale.log_scale, f32[1]{0:T(128)S(6)} %copy.15.imu_bias.bias, ...), custom_call_target="tpu_custom_call" | custom-call | flops 500000000 | bytes 4852736 | tf_op jit(solution)/shard_map/pallas_call | solution.py:268
  14.6 1.1 %collective-permute-start = (bf16[400,1024]{1,0:T(8,128)(2,1)S(1)}, bf16[400,1024]{1,0:T(8,128)(2,1)S(1)}, u32[]{:S(2)}, u32[]{:S(2)}) collective-permute-start(bf16[400,1024]{1,0:T(8,128)(2,1)S(1)} %get-tuple-element.36), channel_id=1, source_target_pairs={{4,0},{8,4},{12,8},{16,12},{20,16},{24,20},{28,24},{0,28},{5,1},{9... | collective-permute-start | bytes 2457608 | tf_op jit(solution)/shard_map/ppermute | solution.py:295
  15.7 0.7 collective-permute-start.1
  16.4 23.2 %collective-permute-done.4.audio_ids = s32[384]{0:T(512)S(1)} collective-permute-done((s32[384]{0:T(512)S(1)}, s32[384]{0:T(512)S(1)}, u32[]{:S(2)}, u32[]{:S(2)}) %collective-permute-start.4) | collective-permute-done | bytes 1568 | tf_op jit(solution)/shard_map/ppermute | solution.py:298
  39.5 0.0 collective-permute-done.3.audio
  39.5 2.0 %shard_map.131 = (f32[1,384]{1,0:T(1,128)S(1)}, f32[384,1024]{1,0:T(8,128)S(1)}, f32[384,1024]{1,0:T(8,128)S(1)}) custom-call(f32[1]{0:T(128)S(6)} %copy.16.audio_log_scale.log_scale, f32[1]{0:T(128)S(6)} %copy.17.audio_bias.bias, bf16[400,1024]{1,0:T(8,128)(2,1)S(1)} %get-tuple-element.34.video, bf16[384,1024]{1,0:T(8,128)(2,1)S(1)} %collective-permute-done.3.audio, ...), custom_call_target="tpu_custom_call" | custom-call | flops 500000000 | bytes 6363136 | tf_op jit(solution)/shard_map/pallas_call | solution.py:268
  41.6 0.1 collective-permute-done.2.other_video
  41.7 1.9 %shard_map.132 = (f32[1,384]{1,0:T(1,128)S(1)}, f32[384,1024]{1,0:T(8,128)S(1)}, bf16[384,1024]{1,0:T(8,128)(2,1)S(1)}, f32[1,384]{1,0:T(1,128)S(1)}) custom-call(f32[1]{0:T(128)S(6)} %copy.16.audio_log_scale.log_scale, f32[1]{0:T(128)S(6)} %copy.17.audio_bias.bias, bf16[400,1024]{1,0:T(8,128)(2,1)S(1)} %collective-permute-done.2.other_video, ...), custom_call_target="tpu_custom_call" | custom-call | flops 500000000 | bytes 6363136 | tf_op jit(solution)/shard_map/pallas_call | solution.py:268
  43.6 3.2 %collective-permute-start.8 = (bf16[384,1024]{1,0:T(8,128)(2,1)S(1)}, bf16[384,1024]{1,0:T(8,128)(2,1)S(1)}, u32[]{:S(2)}, u32[]{:S(2)}) collective-permute-start(bf16[384,1024]{1,0:T(8,128)(2,1)S(1)} %get-tuple-element.53), channel_id=1, source_target_pairs={{0,2},{1,3},{2,0},{3,1},{4,6},{5,7},{6,4},{7,5},{8,10},{9,11},{10,... | collective-permute-start | bytes 2359304 | tf_op jit(solution)/shard_map/ppermute | solution.py:304
  46.8 2.0 %shard_map.133 = (bf16[400,1024]{1,0:T(8,128)(2,1)S(1)}, f32[384,1024]{1,0:T(8,128)S(1)}, f32[1,384]{1,0:T(1,128)S(1)}) custom-call(f32[1]{0:T(128)S(6)} %copy.16.audio_log_scale.log_scale, f32[1]{0:T(128)S(6)} %copy.17.audio_bias.bias, bf16[400,1024]{1,0:T(8,128)(2,1)S(1)} %collective-permute-done.2.other_video, bf16[384,1024]{1,0:T(8,128)(2,1)S(1)} %copy-done, ...), custom_call_target="tpu_custom_call" | custom-call | flops 500000000 | bytes 9511936 | tf_op jit(solution)/shard_map/pallas_call | solution.py:268
  48.9 0.9 %collective-permute-start.7 = (bf16[400,1024]{1,0:T(8,128)(2,1)S(1)}, bf16[400,1024]{1,0:T(8,128)(2,1)S(1)}, u32[]{:S(2)}, u32[]{:S(2)}) collective-permute-start(bf16[400,1024]{1,0:T(8,128)(2,1)S(1)} %get-tuple-element.51), channel_id=1, source_target_pairs={{0,1},{1,0},{2,3},{3,2},{4,5},{5,4},{6,7},{7,6},{8,9},{9,8},{10,11... | collective-permute-start | bytes 2457608 | tf_op jit(solution)/shard_map/ppermute | solution.py:301
  49.8 0.0 collective-permute-done.other_video
  49.8 0.0 collective-permute-done.1.other_imu
  49.8 4.8 %shard_map.134 = (f32[1,384]{1,0:T(1,128)S(1)}, f32[384,1024]{1,0:T(8,128)S(1)}, f32[384,1024]{1,0:T(8,128)S(1)}, bf16[400,1024]{1,0:T(8,128)(2,1)S(1)}, bf16[384,1024]{1,0:T(8,128)(2,1)S(1)}) custom-call(f32[1]{0:T(128)S(6)} %copy.14.imu_log_scale.log_scale, f32[1]{0:T(128)S(6)} %copy.15.imu_bias.bias, bf16[400,1024]{1,0:T(8,128)(2,1)S(1)} %get-tuple-element.34.video, ...), custom_call_target="tpu_custom_call" | custom-call | flops 500000000 | bytes 12848128 | tf_op jit(solution)/shard_map/pallas_call | solution.py:268
  54.6 2.5 %collective-permute-start.6 = (bf16[384,1024]{1,0:T(8,128)(2,1)S(1)}, bf16[384,1024]{1,0:T(8,128)(2,1)S(1)}, u32[]{:S(2)}, u32[]{:S(2)}) collective-permute-start(bf16[384,1024]{1,0:T(8,128)(2,1)S(1)} %get-tuple-element.50), channel_id=1, source_target_pairs={{0,24},{4,28},{8,0},{12,4},{16,8},{20,12},{24,16},{28,20},{1,25},{... | collective-permute-start | bytes 2359304 | tf_op jit(solution)/shard_map/ppermute | solution.py:304
  57.1 0.0 collective-permute-start.5
  57.1 23.4 %collective-permute-done.8.got_audio = bf16[384,1024]{1,0:T(8,128)(2,1)S(1)} collective-permute-done((bf16[384,1024]{1,0:T(8,128)(2,1)S(1)}, bf16[384,1024]{1,0:T(8,128)(2,1)S(1)}, u32[]{:S(2)}, u32[]{:S(2)}) %collective-permute-start.8) | collective-permute-done | bytes 786464 | tf_op jit(solution)/shard_map/ppermute | solution.py:304
  80.5 1.2 %shard_map.135 = (f32[384,1024]{1,0:T(8,128)}, f32[1,384]{1,0:T(1,128)S(1)}) custom-call(bf16[384,1024]{1,0:T(8,128)(2,1)S(1)} %collective-permute-done.8.got_audio, f32[384,1024]{1,0:T(8,128)S(1)} %get-tuple-element.54.audio_in, f32[1,384]{1,0:T(1,128)S(1)} %get-tuple-element.55.loss_in), custom_call_target="tpu_custom_call" | custom-call | flops 5000000000 | tf_op jit(solution)/shard_map/pallas_call | solution.py:253
  81.7 1.7 %collective-permute-done.7.got_video = bf16[400,1024]{1,0:T(8,128)(2,1)S(1)} collective-permute-done((bf16[400,1024]{1,0:T(8,128)(2,1)S(1)}, bf16[400,1024]{1,0:T(8,128)(2,1)S(1)}, u32[]{:S(2)}, u32[]{:S(2)}) %collective-permute-start.7) | collective-permute-done | bytes 819232 | tf_op jit(solution)/shard_map/ppermute | solution.py:301
  83.3 0.2 shard_map.136
  83.6 0.0 collective-permute-done.6.got_imu
  83.6 0.0 collective-permute-done.5.got_video
  83.6 2.3 %shard_map.137 = (f32[384,1024]{1,0:T(8,128)}, f32[384,1024]{1,0:T(8,128)}, f32[384]{0:T(512)}) custom-call(bf16[400,1024]{1,0:T(8,128)(2,1)S(1)} %collective-permute-done.5.got_video, bf16[384,1024]{1,0:T(8,128)(2,1)S(1)} %collective-permute-done.6.got_imu, f32[384,1024]{1,0:T(8,128)S(1)} %get-tuple-element.57.video_in, ...), custom_call_target="tpu_custom_call" | custom-call | flops 500000000 | tf_op jit(solution)/shard_map/pallas_call | solution.py:253
Async XLA Ops:
  0.6 10.1 %copy-start = (bf16[384,1024]{1,0:T(8,128)(2,1)S(1)}, bf16[384,1024]{1,0:T(8,128)(2,1)}, u32[]{:S(2)}) copy-start(bf16[384,1024]{1,0:T(8,128)(2,1)} %audio.3) | copy-start | bytes 2359300
  0.6 7.2 %copy-start.1 = (s32[384]{0:T(512)S(1)}, s32[384]{0:T(512)}, u32[]{:S(2)}) copy-start(s32[384]{0:T(512)} %audio_ids.3) | copy-start | bytes 4612
  0.7 38.9 %collective-permute-start.3 = (bf16[384,1024]{1,0:T(8,128)(2,1)}, bf16[384,1024]{1,0:T(8,128)(2,1)S(1)}, u32[]{:S(2)}, u32[]{:S(2)}) collective-permute-start(bf16[384,1024]{1,0:T(8,128)(2,1)} %audio.3), channel_id=1, source_target_pairs={{2,0},{3,1},{0,2},{1,3},{6,4},{7,5},{4,6},{5,7},{10,8},{11,9},{8,1... | collective-permute-start | bytes 2359304 | tf_op jit(solution)/shard_map/ppermute | solution.py:298
  6.2 35.5 %collective-permute-start.2 = (bf16[400,1024]{1,0:T(8,128)(2,1)S(1)}, bf16[400,1024]{1,0:T(8,128)(2,1)S(1)}, u32[]{:S(2)}, u32[]{:S(2)}) collective-permute-start(bf16[400,1024]{1,0:T(8,128)(2,1)S(1)} %get-tuple-element.34.video), channel_id=1, source_target_pairs={{1,0},{0,1},{3,2},{2,3},{5,4},{4,5},{7,6},{6,7},{9,8},{8,9},{11,10... | collective-permute-start | bytes 2457608 | tf_op jit(solution)/shard_map/ppermute | solution.py:295
  7.8 31.7 %collective-permute-start.4 = (s32[384]{0:T(512)S(1)}, s32[384]{0:T(512)S(1)}, u32[]{:S(2)}, u32[]{:S(2)}) collective-permute-start(s32[384]{0:T(512)S(1)} %copy-done.1), channel_id=1, source_target_pairs={{2,0},{3,1},{0,2},{1,3},{6,4},{7,5},{4,6},{5,7},{10,8},{11,9},{8,1... | collective-permute-start | bytes 4616 | tf_op jit(solution)/shard_map/ppermute | solution.py:298
  14.6 35.2 %collective-permute-start = (bf16[400,1024]{1,0:T(8,128)(2,1)S(1)}, bf16[400,1024]{1,0:T(8,128)(2,1)S(1)}, u32[]{:S(2)}, u32[]{:S(2)}) collective-permute-start(bf16[400,1024]{1,0:T(8,128)(2,1)S(1)} %get-tuple-element.36), channel_id=1, source_target_pairs={{4,0},{8,4},{12,8},{16,12},{20,16},{24,20},{28,24},{0,28},{5,1},{9... | collective-permute-start | bytes 2457608 | tf_op jit(solution)/shard_map/ppermute | solution.py:295
  15.7 34.1 %collective-permute-start.1 = (bf16[400,1024]{1,0:T(8,128)(2,1)S(1)}, bf16[400,1024]{1,0:T(8,128)(2,1)S(1)}, u32[]{:S(2)}, u32[]{:S(2)}) collective-permute-start(bf16[400,1024]{1,0:T(8,128)(2,1)S(1)} %get-tuple-element.37), channel_id=1, source_target_pairs={{24,0},{28,4},{0,8},{4,12},{8,16},{12,20},{16,24},{20,28},{25,1},{... | collective-permute-start | bytes 2457608 | tf_op jit(solution)/shard_map/ppermute | solution.py:298
  43.6 36.8 %collective-permute-start.8 = (bf16[384,1024]{1,0:T(8,128)(2,1)S(1)}, bf16[384,1024]{1,0:T(8,128)(2,1)S(1)}, u32[]{:S(2)}, u32[]{:S(2)}) collective-permute-start(bf16[384,1024]{1,0:T(8,128)(2,1)S(1)} %get-tuple-element.53), channel_id=1, source_target_pairs={{0,2},{1,3},{2,0},{3,1},{4,6},{5,7},{6,4},{7,5},{8,10},{9,11},{10,... | collective-permute-start | bytes 2359304 | tf_op jit(solution)/shard_map/ppermute | solution.py:304
  48.9 34.5 %collective-permute-start.7 = (bf16[400,1024]{1,0:T(8,128)(2,1)S(1)}, bf16[400,1024]{1,0:T(8,128)(2,1)S(1)}, u32[]{:S(2)}, u32[]{:S(2)}) collective-permute-start(bf16[400,1024]{1,0:T(8,128)(2,1)S(1)} %get-tuple-element.51), channel_id=1, source_target_pairs={{0,1},{1,0},{2,3},{3,2},{4,5},{5,4},{6,7},{7,6},{8,9},{9,8},{10,11... | collective-permute-start | bytes 2457608 | tf_op jit(solution)/shard_map/ppermute | solution.py:301
  54.6 29.0 %collective-permute-start.6 = (bf16[384,1024]{1,0:T(8,128)(2,1)S(1)}, bf16[384,1024]{1,0:T(8,128)(2,1)S(1)}, u32[]{:S(2)}, u32[]{:S(2)}) collective-permute-start(bf16[384,1024]{1,0:T(8,128)(2,1)S(1)} %get-tuple-element.50), channel_id=1, source_target_pairs={{0,24},{4,28},{8,0},{12,4},{16,8},{20,12},{24,16},{28,20},{1,25},{... | collective-permute-start | bytes 2359304 | tf_op jit(solution)/shard_map/ppermute | solution.py:304
  57.1 26.5 %collective-permute-start.5 = (bf16[400,1024]{1,0:T(8,128)(2,1)S(1)}, bf16[400,1024]{1,0:T(8,128)(2,1)S(1)}, u32[]{:S(2)}, u32[]{:S(2)}) collective-permute-start(bf16[400,1024]{1,0:T(8,128)(2,1)S(1)} %get-tuple-element.49), channel_id=1, source_target_pairs={{0,4},{4,8},{8,12},{12,16},{16,20},{20,24},{24,28},{28,0},{1,5},{5... | collective-permute-start | bytes 2457608 | tf_op jit(solution)/shard_map/ppermute | solution.py:301
where the time goes:
time: 86.2 us; the launch traced here: 86.1 us
  waiting for transfers between devices  48.3 us (56%)
  Pallas kernels  19.7 us (23%)
  starting transfers between devices  14.5 us (17%)
  between operations  3.49 us (4%)
    ppermute x2, waiting for transfers between devices, return_partner(): return lax.ppermute(block, self.axis, [(b, a) for a, b in self.partner])  23.4 us
    ppermute x3, waiting for transfers between devices, bring_partner(): return lax.ppermute(block, self.axis, self.partner)  23.2 us
    pallas_call x5, Pallas kernels, call(): pl.pallas_call(kernel, out_shape=[jax.ShapeDtypeStruct(*out) for out in o...  14.5 us
    ppermute x2, starting transfers between devices, return_partner(): return lax.ppermute(block, self.axis, [(b, a) for a, b in self.partner])  5.71 us
    ppermute x3, starting transfers between devices, bring_partner(): return lax.ppermute(block, self.axis, self.partner)  5.13 us
    pallas_call x3, Pallas kernels, summed(): pl.pallas_call(kernel, out_shape=[jax.ShapeDtypeStruct(*out) for out in o...  3.75 us
    ppermute x2, starting transfers between devices, bring_video(): return lax.ppermute(block, self.axis, self.video)  2.74 us
  transfers between devices with their start and end apart: 9, of which 4 were waited for; matrix products, arithmetic and copies ran while one was open for 0% of the time, Pallas kernels for 20%

commit v1 on v0

--- a/solution.py
+++ b/solution.py
@@ -12,8 +12,8 @@
 TAG_ROWS = 16
 TAG_BASE = 256
 COSTS = {
-    "own": 0.5e9, "col_own": 0.5e9, "row": 0.5e9, "col_far": 0.5e9,
-    "col_near": 0.5e9, "row_sum": 0.5e9, "audio_sum": 5e9, "video_sum": 20e9,
+    "own": 0.5e9, "own_far": 0.5e9, "far": 0.5e9, "near": 0.5e9, "row": 0.5e9, "late": 0.01e9,
+    "audio_sum": 5e9, "video_sum": 20e9, "row_sum": 0.5e9,
 }
 
 F32 = jnp.float32
@@ -145,9 +145,41 @@
     packed[rows:, rows:] = jnp.zeros((TAG_ROWS, packed.shape[1] - rows), BF16)
 
 
+def own_far_kernel(
+    log_scale, bias, video, audio, audio_ids, loss_in, loss, weights, products
+):
+    scalars = (log_scale, bias)
+    loss[...] = loss_in[...] + meet(video, (audio, audio_ids), scalars, products, weights)
+
+
+def far_kernel(
+    log_scale, bias, video, other_video, audio, audio_ids, own_weights, loss_in,
+    loss, other_loss, sums, weights, products,
+):
+    loss[...] = loss_in[...]
+    other_loss[...] = meet(other_video, (audio, audio_ids), (log_scale, bias), products, weights)
+    for part in column_parts(video):
+        both = to_partner(own_weights, video, part) + to_partner(weights, other_video, part)
+        sums[:, part] = both.astype(BF16)
+
+
+def near_kernel(
+    log_scale, bias, other_video, audio, audio_ids, far_audio, far_weights, other_loss_in, loss_in,
+    other_grad, weights, loss, products,
+):
+    audio = (audio, audio_ids)
+    rows = weights.shape[0]
+    loss[...] = loss_in[...]
+    losses = meet(other_video, audio, (log_scale, bias), products, weights)
+    put_losses(other_loss_in[...] + losses, other_grad)
+    for part in column_parts(other_video):
+        both = to_video(weights, audio, part) + to_video(far_weights, far_audio, part)
+        other_grad[:rows, part] = both.astype(BF16)
+
+
 def row_kernel(
-    log_scale, bias, video, other_video, imu, other_imu, loss_in, video_in, grad_in,
-    loss, video_grad, grad, other_grad, sums, products, weights, other_weights, near_weights,
+    log_scale, bias, video, other_video, imu, other_imu, loss_in,
+    loss, other_grad, sums, weights, near_weights, products, other_weights,
 ):
     scalars = (log_scale, bias)
     rows = sums.shape[0]
@@ -160,46 +192,19 @@
         other_grad[:rows, part] = other_sum.astype(BF16)
         both = to_partner(weights, video, part) + to_partner(other_weights, other_video, part)
         sums[:, part] = both.astype(BF16)
-        grad[:, part] = grad_in[:, part] + to_partner(near_weights, other_video, part)
-        video_grad[:, part] = video_in[:, part] + to_video(weights, other_imu, part)
-
-
-def col_own_kernel(
-    log_scale, bias, video, audio, audio_ids, loss_in, video_in,
-    loss, video_grad, sums, products, weights,
-):
-    audio = (audio, audio_ids)
-    loss[...] = loss_in[...] + meet(video, audio, (log_scale, bias), products, weights)
-    for part in column_parts(video):
-        video_grad[:, part] = video_in[:, part] + to_video(weights, audio, part)
-        sums[:, part] = to_partner(weights, video, part)
-
-
-def col_far_kernel(
-    log_scale, bias, other_video, audio, audio_ids, sums_in, loss_in,
-    other_loss, other_grad, sums, loss, products, weights,
+
+
+def late_kernel(
+    far_audio, far_weights, col_video, near_weights, row_imu, row_weights, row_video,
+    row_near_weights, video_in, audio_in, imu_in, loss_in,
+    video_grad, audio_grad, imu_grad, loss,
 ):
     loss[...] = loss_in[...]
-    audio = (audio, audio_ids)
-    other_loss[...] = meet(other_video, audio, (log_scale, bias), products, weights)
-    for part in column_parts(other_video):
-        sums[:, part] = (sums_in[:, part] + to_partner(weights, other_video, part)).astype(BF16)
-        other_grad[:, part] = to_video(weights, audio, part)
-
-
-def col_near_kernel(
-    log_scale, bias, other_video, audio, audio_ids, other_loss_in, other_in, grad_in, loss_in,
-    other_grad, grad, loss, products, weights,
-):
-    loss[...] = loss_in[...]
-    audio = (audio, audio_ids)
-    rows = grad.shape[0]
-    losses = meet(other_video, audio, (log_scale, bias), products, weights)
-    put_losses(other_loss_in[...] + losses, other_grad)
-    for part in column_parts(other_video):
-        other_sum = other_in[:, part] + to_video(weights, audio, part)
-        other_grad[:rows, part] = other_sum.astype(BF16)
-        grad[:, part] = grad_in[:, part] + to_partner(weights, other_video, part)
+    for part in column_parts(video_grad):
+        video_sum = to_video(far_weights, far_audio, part) + to_video(row_weights, row_imu, part)
+        video_grad[:, part] = video_in[:, part] + video_sum
+        audio_grad[:, part] = audio_in[:, part] + to_partner(near_weights, col_video, part)
+        imu_grad[:, part] = imu_in[:, part] + to_partner(row_near_weights, row_video, part)
 
 
 def added(parts, out, buffer, done):
@@ -262,9 +267,10 @@
     )(*args)
 
 
-def call(kernel, outs, scalars, args, rows, weights=1, cost=0):
+def call(kernel, outs, scalars, args, rows, weights=1, cost=0, meets=True):
     smem, vmem = pl.BlockSpec(memory_space=pltpu.SMEM), pl.BlockSpec(memory_space=pltpu.VMEM)
     scratch = [pltpu.VMEM((rows, rows), F32)] + [pltpu.VMEM((rows, rows), BF16)] * weights
+    scratch = scratch if meets else []
     return pl.pallas_call(
         kernel,
         out_shape=[jax.ShapeDtypeStruct(*out) for out in outs],
@@ -328,39 +334,49 @@
     )
     row_video = along_row.bring_video(video_on)
     row_imu = along_row.bring_partner(imu_on)
-    loss, video_grad, sums = call(
-        col_own_kernel,
-        [line, square, square],
+    tile = ((rows, rows), BF16)
+    loss, far_weights = call(
+        own_far_kernel,
+        [line, tile],
         of_audio,
-        (video, *col_audio, loss, video_grad),
-        rows, 1, COSTS["col_own"],
-    )
-    col_loss, col_grad, sums, loss = call(
-        col_far_kernel,
-        [line, square, narrow, line],
+        (video, *col_audio, loss),
+        rows, 0, COSTS["own_far"],
+    )
+    loss, col_loss, sums, far_col_weights = call(
+        far_kernel,
+        [line, line, narrow, tile],
         of_audio,
-        (col_video, *col_audio, sums, loss),
-        rows, 1, COSTS["col_far"],
+        (video, col_video, *col_audio, far_weights, loss),
+        rows, 0, COSTS["far"],
     )
     got_audio = along_col.return_partner(sums)
-    col_grad, audio_grad, loss = call(
-        col_near_kernel,
-        [packed, square, line],
+    col_grad, near_weights, loss = call(
+        near_kernel,
+        [packed, tile, line],
         of_audio,
-        (col_video, *audio, col_loss, col_grad, audio_grad, loss),
-        rows, 1, COSTS["col_near"],
+        (col_video, *audio, col_audio[0], far_col_weights, col_loss, loss),
+        rows, 0, COSTS["near"],
     )
     got_col = along_col.return_video(col_grad)
-
-    loss, video_grad, imu_grad, row_grad, row_sums = call(
+    loss, row_grad, sums, row_weights, row_near_weights = call(
         row_kernel,
-        [line, square, square, packed, narrow],
+        [line, packed, narrow, tile, tile],
         of_imu,
-        (video, row_video, imu, row_imu, loss, video_grad, imu_grad),
-        rows, 3, COSTS["row"],
+        (video, row_video, imu, row_imu, loss),
+        rows, 1, COSTS["row"],
     )
     got_row = along_row.return_video(row_grad)
-    got_imu = along_row.return_partner(row_sums)
+    got_imu = along_row.return_partner(sums)
+    video_grad, audio_grad, imu_grad, loss = call(
+        late_kernel,
+        [square, square, square, line],
+        (),
+        (
+            col_audio[0], far_weights, col_video, near_weights, row_imu, row_weights, row_video,
+            row_near_weights, video_grad, audio_grad, imu_grad, loss,
+        ),
+        rows, 0, COSTS["late"], False,
+    )
 
     hbm, vmem = pltpu.HBM, pltpu.VMEM
     audio_grad, loss = summed(

time: 86.2 us -> 84.9 us (0.985)
  starting transfers between devices: 14.5 us -> 13.4 us
    ppermute x2, starting transfers between devices: 5.71 us -> 4.69 us  [return_partner(): return lax.ppermute(block, self.axis, [(b, a) for a, b in self.partner])]
    ppermute x2, waiting for transfers between devices: 0.14 us -> 1.16 us  [bring_video(): return lax.ppermute(block, self.axis, self.video)]
    pallas_call x5 -> x6, Pallas kernels: 14.5 us -> 14.3 us  [call(): pl.pallas_call(kernel, out_shape=[jax.ShapeDtypeStruct(*out) for out in o...]
where the time goes in v1:
time: 84.9 us; the launch traced here: 84.7 us
  waiting for transfers between devices  48.6 us (57%)
  Pallas kernels  19.4 us (23%)
  starting transfers between devices  13.4 us (16%)
  between operations  3.33 us (4%)
    ppermute x3, waiting for transfers between devices, bring_partner(): return lax.ppermute(block, self.axis, self.partner)  23.3 us
    ppermute x2, waiting for transfers between devices, return_partner(): return lax.ppermute(block, self.axis, [(b, a) for a, b in self.partner])  22.7 us
    pallas_call x6, Pallas kernels, call(): pl.pallas_call(kernel, out_shape=[jax.ShapeDtypeStruct(*out) for out in o...  14.3 us
    ppermute x3, starting transfers between devices, bring_partner(): return lax.ppermute(block, self.axis, self.partner)  4.95 us
    ppermute x2, starting transfers between devices, return_partner(): return lax.ppermute(block, self.axis, [(b, a) for a, b in self.partner])  4.69 us
    pallas_call x3, Pallas kernels, summed(): pl.pallas_call(kernel, out_shape=[jax.ShapeDtypeStruct(*out) for out in o...  3.69 us
    ppermute x2, starting transfers between devices, bring_video(): return lax.ppermute(block, self.axis, self.video)  2.75 us
  transfers between devices with their start and end apart: 9, of which 4 were waited for; matrix products, arithmetic and copies ran while one was open for 0% of the time, Pallas kernels for 20%

profile of v1, /device:TPU:0, one launch (start us, length us, event | category | flops | bytes accessed | tf_op | source)
XLA Modules:
  0.0 84.7 jit_solution(4860057539902990392)
XLA Ops:
  0.6 0.0 copy-start
  0.6 0.0 copy-start.1
  0.7 4.1 %collective-permute-start.3 = (bf16[384,1024]{1,0:T(8,128)(2,1)}, bf16[384,1024]{1,0:T(8,128)(2,1)S(1)}, u32[]{:S(2)}, u32[]{:S(2)}) collective-permute-start(bf16[384,1024]{1,0:T(8,128)(2,1)} %audio.3), channel_id=1, source_target_pairs={{2,0},{3,1},{0,2},{1,3},{6,4},{7,5},{4,6},{5,7},{10,8},{11,9},{8,1... | collective-permute-start | bytes 2359304 | tf_op jit(solution)/shard_map/ppermute | solution.py:304
  4.8 1.4 %shard_map.129 = (bf16[400,1024]{1,0:T(8,128)(2,1)S(1)}, bf16[400,1024]{1,0:T(8,128)(2,1)S(1)}) custom-call(bf16[384,1024]{1,0:T(8,128)(2,1)} %refs_0_.1, bf16[384,1024]{1,0:T(8,128)(2,1)} %refs_1_.1, s32[384]{0:T(512)} %refs_2_.1, s32[384]{0:T(512)} %refs_3_.1), custom_call_target="tpu_custom_call" | custom-call | tf_op jit(solution)/shard_map/pallas_call | solution.py:52
  6.2 1.6 %collective-permute-start.2 = (bf16[400,1024]{1,0:T(8,128)(2,1)S(1)}, bf16[400,1024]{1,0:T(8,128)(2,1)S(1)}, u32[]{:S(2)}, u32[]{:S(2)}) collective-permute-start(bf16[400,1024]{1,0:T(8,128)(2,1)S(1)} %get-tuple-element.37.video), channel_id=1, source_target_pairs={{1,0},{0,1},{3,2},{2,3},{5,4},{4,5},{7,6},{6,7},{9,8},{8,9},{11,10... | collective-permute-start | bytes 2457608 | tf_op jit(solution)/shard_map/ppermute | solution.py:301
  7.8 0.0 copy-done.1
  7.8 0.3 collective-permute-start.4
  10.8 0.0 copy-done
  10.8 3.8 %shard_map.130 = (f32[1,384]{1,0:T(1,128)S(1)}, f32[384,1024]{1,0:T(8,128)S(1)}, f32[384,1024]{1,0:T(8,128)S(1)}, f32[384,1024]{1,0:T(8,128)S(1)}, bf16[400,1024...) custom-call(f32[1]{0:T(128)S(6)} %copy.14.imu_log_scale.log_scale, f32[1]{0:T(128)S(6)} %copy.15.imu_bias.bias, ...), custom_call_target="tpu_custom_call" | custom-call | flops 500000000 | bytes 4852736 | tf_op jit(solution)/shard_map/pallas_call | solution.py:274
  14.6 1.1 %collective-permute-start = (bf16[400,1024]{1,0:T(8,128)(2,1)S(1)}, bf16[400,1024]{1,0:T(8,128)(2,1)S(1)}, u32[]{:S(2)}, u32[]{:S(2)}) collective-permute-start(bf16[400,1024]{1,0:T(8,128)(2,1)S(1)} %get-tuple-element.39), channel_id=1, source_target_pairs={{4,0},{8,4},{12,8},{16,12},{20,16},{24,20},{28,24},{0,28},{5,1},{9... | collective-permute-start | bytes 2457608 | tf_op jit(solution)/shard_map/ppermute | solution.py:301
  15.7 0.5 collective-permute-start.1
  16.2 23.3 %collective-permute-done.4.audio_ids = s32[384]{0:T(512)S(1)} collective-permute-done((s32[384]{0:T(512)S(1)}, s32[384]{0:T(512)S(1)}, u32[]{:S(2)}, u32[]{:S(2)}) %collective-permute-start.4) | collective-permute-done | bytes 1568 | tf_op jit(solution)/shard_map/ppermute | solution.py:304
  39.5 0.0 collective-permute-done.3.audio.far_audio
  39.5 1.0 %shard_map.131 = (f32[1,384]{1,0:T(1,128)S(1)}, bf16[384,384]{1,0:T(8,128)(2,1)S(1)}) custom-call(f32[1]{0:T(128)S(6)} %copy.16.audio_log_scale.log_scale, f32[1]{0:T(128)S(6)} %copy.17.audio_bias.bias, bf16[400,1024]{1,0:T(8,128)(2,1)S(1)} %get-tuple-element.37.video, bf16[384,1024]{1,0:T(8,128)(2,1)S(1)} %collective-permute-done.3.audio.far_audio, ...), custom_call_target="tpu_custom_call" | custom-call | flops 500000000 | bytes 3217408 | tf_op jit(solution)/shard_map/pallas_call | solution.py:274
  40.5 1.2 %collective-permute-done.2.other_video.col_video = bf16[400,1024]{1,0:T(8,128)(2,1)S(1)} collective-permute-done((bf16[400,1024]{1,0:T(8,128)(2,1)S(1)}, bf16[400,1024]{1,0:T(8,128)(2,1)S(1)}, u32[]{:S(2)}, u32[]{:S(2)}) %collective-permute-start.2) | collective-permute-done | bytes 819232 | tf_op jit(solution)/shard_map/ppermute | solution.py:301
  41.7 1.9 %shard_map.132 = (f32[1,384]{1,0:T(1,128)S(1)}, f32[1,384]{1,0:T(1,128)S(1)}, bf16[384,1024]{1,0:T(8,128)(2,1)S(1)}, bf16[384,384]{1,0:T(8,128)(2,1)S(1)}) custom-call(f32[1]{0:T(128)S(6)} %copy.16.audio_log_scale.log_scale, f32[1]{0:T(128)S(6)} %copy.17.audio_bias.bias, bf16[400,1024]{1,0:T(8,128)(2,1)S(1)} %get-tuple-element.37.video, ...), custom_call_target="tpu_custom_call" | custom-call | flops 500000000 | bytes 5445632 | tf_op jit(solution)/shard_map/pallas_call | solution.py:274
  43.6 2.2 %collective-permute-start.8 = (bf16[384,1024]{1,0:T(8,128)(2,1)S(1)}, bf16[384,1024]{1,0:T(8,128)(2,1)S(1)}, u32[]{:S(2)}, u32[]{:S(2)}) collective-permute-start(bf16[384,1024]{1,0:T(8,128)(2,1)S(1)} %get-tuple-element.59), channel_id=1, source_target_pairs={{0,2},{1,3},{2,0},{3,1},{4,6},{5,7},{6,4},{7,5},{8,10},{9,11},{10,... | collective-permute-start | bytes 2359304 | tf_op jit(solution)/shard_map/ppermute | solution.py:310
  45.8 1.8 %shard_map.133 = (bf16[400,1024]{1,0:T(8,128)(2,1)S(1)}, bf16[384,384]{1,0:T(8,128)(2,1)S(1)}, f32[1,384]{1,0:T(1,128)S(1)}) custom-call(f32[1]{0:T(128)S(6)} %copy.16.audio_log_scale.log_scale, f32[1]{0:T(128)S(6)} %copy.17.audio_bias.bias, bf16[400,1024]{1,0:T(8,128)(2,1)S(1)} %collective-permute-done.2.other_video.col_video, ...), custom_call_target="tpu_custom_call" | custom-call | flops 500000000 | bytes 5383168 | tf_op jit(solution)/shard_map/pallas_call | solution.py:274
  47.6 1.0 %collective-permute-start.7 = (bf16[400,1024]{1,0:T(8,128)(2,1)S(1)}, bf16[400,1024]{1,0:T(8,128)(2,1)S(1)}, u32[]{:S(2)}, u32[]{:S(2)}) collective-permute-start(bf16[400,1024]{1,0:T(8,128)(2,1)S(1)} %get-tuple-element.50), channel_id=1, source_target_pairs={{0,1},{1,0},{2,3},{3,2},{4,5},{5,4},{6,7},{7,6},{8,9},{9,8},{10,11... | collective-permute-start | bytes 2457608 | tf_op jit(solution)/shard_map/ppermute | solution.py:307
  48.5 0.0 collective-permute-done.other_video.row_video
  48.5 0.0 collective-permute-done.1.other_imu.row_imu
  48.5 4.0 %shard_map.134 = (f32[1,384]{1,0:T(1,128)S(1)}, bf16[400,1024]{1,0:T(8,128)(2,1)S(1)}, bf16[384,1024]{1,0:T(8,128)(2,1)S(1)}, bf16[384,384]{1,0:T(8,128)(2,1)S(1)}, bf16[384,384]{1,0:T(8,128)(2,1)S(1)}) custom-call(f32[1]{0:T(128)S(6)} %copy.14.imu_log_scale.log_scale, f32[1]{0:T(128)S(6)} %copy.15.imu_bias.bias, ...), custom_call_target="tpu_custom_call" | custom-call | flops 500000000 | bytes 6556672 | tf_op jit(solution)/shard_map/pallas_call | solution.py:274
  52.5 2.5 %collective-permute-start.6 = (bf16[384,1024]{1,0:T(8,128)(2,1)S(1)}, bf16[384,1024]{1,0:T(8,128)(2,1)S(1)}, u32[]{:S(2)}, u32[]{:S(2)}) collective-permute-start(bf16[384,1024]{1,0:T(8,128)(2,1)S(1)} %get-tuple-element.49), channel_id=1, source_target_pairs={{0,24},{4,28},{8,0},{12,4},{16,8},{20,12},{24,16},{28,20},{1,25},{... | collective-permute-start | bytes 2359304 | tf_op jit(solution)/shard_map/ppermute | solution.py:310
  55.0 0.0 collective-permute-start.5
  55.0 1.9 %shard_map.135 = (f32[384,1024]{1,0:T(8,128)S(1)}, f32[384,1024]{1,0:T(8,128)S(1)}, f32[384,1024]{1,0:T(8,128)S(1)}, f32[1,384]{1,0:T(1,128)S(1)}) custom-call(bf16[384,1024]{1,0:T(8,128)(2,1)S(1)} %collective-permute-done.3.audio.far_audio, bf16[384,384]{1,0:T(8,128)(2,1)S(1)} %get-tuple-element.42.own_weights.far_weights, ...), custom_call_target="tpu_custom_call" | custom-call | flops 10000000 | bytes 18287616 | tf_op jit(solution)/shard_map/pallas_call | solution.py:274
  56.9 22.7 %collective-permute-done.8.got_audio = bf16[384,1024]{1,0:T(8,128)(2,1)S(1)} collective-permute-done((bf16[384,1024]{1,0:T(8,128)(2,1)S(1)}, bf16[384,1024]{1,0:T(8,128)(2,1)S(1)}, u32[]{:S(2)}, u32[]{:S(2)}) %collective-permute-start.8) | collective-permute-done | bytes 786464 | tf_op jit(solution)/shard_map/ppermute | solution.py:310
  79.6 1.2 %shard_map.136 = (f32[384,1024]{1,0:T(8,128)}, f32[1,384]{1,0:T(1,128)S(1)}) custom-call(bf16[384,1024]{1,0:T(8,128)(2,1)S(1)} %collective-permute-done.8.got_audio, f32[384,1024]{1,0:T(8,128)S(1)} %get-tuple-element.60.audio_in, f32[1,384]{1,0:T(1,128)S(1)} %get-tuple-element.61.loss_in), custom_call_target="tpu_custom_call" | custom-call | flops 5000000000 | tf_op jit(solution)/shard_map/pallas_call | solution.py:258
  80.8 1.4 %collective-permute-done.7.got_video = bf16[400,1024]{1,0:T(8,128)(2,1)S(1)} collective-permute-done((bf16[400,1024]{1,0:T(8,128)(2,1)S(1)}, bf16[400,1024]{1,0:T(8,128)(2,1)S(1)}, u32[]{:S(2)}, u32[]{:S(2)}) %collective-permute-start.7) | collective-permute-done | bytes 819232 | tf_op jit(solution)/shard_map/ppermute | solution.py:307
  82.2 0.1 shard_map.137
  82.4 0.0 collective-permute-done.6.got_imu
  82.4 0.0 collective-permute-done.5.got_video
  82.4 2.3 %shard_map.138 = (f32[384,1024]{1,0:T(8,128)}, f32[384,1024]{1,0:T(8,128)}, f32[384]{0:T(512)}) custom-call(bf16[400,1024]{1,0:T(8,128)(2,1)S(1)} %collective-permute-done.5.got_video, bf16[384,1024]{1,0:T(8,128)(2,1)S(1)} %collective-permute-done.6.got_imu, f32[384,1024]{1,0:T(8,128)S(1)} %get-tuple-element.63.video_in, ...), custom_call_target="tpu_custom_call" | custom-call | flops 500000000 | tf_op jit(solution)/shard_map/pallas_call | solution.py:258
Async XLA Ops:
  0.6 10.1 %copy-start = (bf16[384,1024]{1,0:T(8,128)(2,1)S(1)}, bf16[384,1024]{1,0:T(8,128)(2,1)}, u32[]{:S(2)}) copy-start(bf16[384,1024]{1,0:T(8,128)(2,1)} %audio.3) | copy-start | bytes 2359300
  0.6 7.2 %copy-start.1 = (s32[384]{0:T(512)S(1)}, s32[384]{0:T(512)}, u32[]{:S(2)}) copy-start(s32[384]{0:T(512)} %audio_ids.3) | copy-start | bytes 4612
  0.7 38.9 %collective-permute-start.3 = (bf16[384,1024]{1,0:T(8,128)(2,1)}, bf16[384,1024]{1,0:T(8,128)(2,1)S(1)}, u32[]{:S(2)}, u32[]{:S(2)}) collective-permute-start(bf16[384,1024]{1,0:T(8,128)(2,1)} %audio.3), channel_id=1, source_target_pairs={{2,0},{3,1},{0,2},{1,3},{6,4},{7,5},{4,6},{5,7},{10,8},{11,9},{8,1... | collective-permute-start | bytes 2359304 | tf_op jit(solution)/shard_map/ppermute | solution.py:304
  6.2 35.5 %collective-permute-start.2 = (bf16[400,1024]{1,0:T(8,128)(2,1)S(1)}, bf16[400,1024]{1,0:T(8,128)(2,1)S(1)}, u32[]{:S(2)}, u32[]{:S(2)}) collective-permute-start(bf16[400,1024]{1,0:T(8,128)(2,1)S(1)} %get-tuple-element.37.video), channel_id=1, source_target_pairs={{1,0},{0,1},{3,2},{2,3},{5,4},{4,5},{7,6},{6,7},{9,8},{8,9},{11,10... | collective-permute-start | bytes 2457608 | tf_op jit(solution)/shard_map/ppermute | solution.py:301
  7.8 31.7 %collective-permute-start.4 = (s32[384]{0:T(512)S(1)}, s32[384]{0:T(512)S(1)}, u32[]{:S(2)}, u32[]{:S(2)}) collective-permute-start(s32[384]{0:T(512)S(1)} %copy-done.1), channel_id=1, source_target_pairs={{2,0},{3,1},{0,2},{1,3},{6,4},{7,5},{4,6},{5,7},{10,8},{11,9},{8,1... | collective-permute-start | bytes 4616 | tf_op jit(solution)/shard_map/ppermute | solution.py:304
  14.6 34.0 %collective-permute-start = (bf16[400,1024]{1,0:T(8,128)(2,1)S(1)}, bf16[400,1024]{1,0:T(8,128)(2,1)S(1)}, u32[]{:S(2)}, u32[]{:S(2)}) collective-permute-start(bf16[400,1024]{1,0:T(8,128)(2,1)S(1)} %get-tuple-element.39), channel_id=1, source_target_pairs={{4,0},{8,4},{12,8},{16,12},{20,16},{24,20},{28,24},{0,28},{5,1},{9... | collective-permute-start | bytes 2457608 | tf_op jit(solution)/shard_map/ppermute | solution.py:301
  15.7 32.9 %collective-permute-start.1 = (bf16[400,1024]{1,0:T(8,128)(2,1)S(1)}, bf16[400,1024]{1,0:T(8,128)(2,1)S(1)}, u32[]{:S(2)}, u32[]{:S(2)}) collective-permute-start(bf16[400,1024]{1,0:T(8,128)(2,1)S(1)} %get-tuple-element.40), channel_id=1, source_target_pairs={{24,0},{28,4},{0,8},{4,12},{8,16},{12,20},{16,24},{20,28},{25,1},{... | collective-permute-start | bytes 2457608 | tf_op jit(solution)/shard_map/ppermute | solution.py:304
  43.6 36.0 %collective-permute-start.8 = (bf16[384,1024]{1,0:T(8,128)(2,1)S(1)}, bf16[384,1024]{1,0:T(8,128)(2,1)S(1)}, u32[]{:S(2)}, u32[]{:S(2)}) collective-permute-start(bf16[384,1024]{1,0:T(8,128)(2,1)S(1)} %get-tuple-element.59), channel_id=1, source_target_pairs={{0,2},{1,3},{2,0},{3,1},{4,6},{5,7},{6,4},{7,5},{8,10},{9,11},{10,... | collective-permute-start | bytes 2359304 | tf_op jit(solution)/shard_map/ppermute | solution.py:310
  47.6 34.7 %collective-permute-start.7 = (bf16[400,1024]{1,0:T(8,128)(2,1)S(1)}, bf16[400,1024]{1,0:T(8,128)(2,1)S(1)}, u32[]{:S(2)}, u32[]{:S(2)}) collective-permute-start(bf16[400,1024]{1,0:T(8,128)(2,1)S(1)} %get-tuple-element.50), channel_id=1, source_target_pairs={{0,1},{1,0},{2,3},{3,2},{4,5},{5,4},{6,7},{7,6},{8,9},{9,8},{10,11... | collective-permute-start | bytes 2457608 | tf_op jit(solution)/shard_map/ppermute | solution.py:307
  52.5 29.9 %collective-permute-start.6 = (bf16[384,1024]{1,0:T(8,128)(2,1)S(1)}, bf16[384,1024]{1,0:T(8,128)(2,1)S(1)}, u32[]{:S(2)}, u32[]{:S(2)}) collective-permute-start(bf16[384,1024]{1,0:T(8,128)(2,1)S(1)} %get-tuple-element.49), channel_id=1, source_target_pairs={{0,24},{4,28},{8,0},{12,4},{16,8},{20,12},{24,16},{28,20},{1,25},{... | collective-permute-start | bytes 2359304 | tf_op jit(solution)/shard_map/ppermute | solution.py:310
  55.0 27.4 %collective-permute-start.5 = (bf16[400,1024]{1,0:T(8,128)(2,1)S(1)}, bf16[400,1024]{1,0:T(8,128)(2,1)S(1)}, u32[]{:S(2)}, u32[]{:S(2)}) collective-permute-start(bf16[400,1024]{1,0:T(8,128)(2,1)S(1)} %get-tuple-element.48), channel_id=1, source_target_pairs={{0,4},{4,8},{8,12},{12,16},{16,20},{20,24},{24,28},{28,0},{1,5},{5... | collective-permute-start | bytes 2457608 | tf_op jit(solution)/shard_map/ppermute | solution.py:307

commit v2 on v1

--- a/solution.py
+++ b/solution.py
@@ -13,7 +13,7 @@
 TAG_BASE = 256
 COSTS = {
     "own": 0.5e9, "own_far": 0.5e9, "far": 0.5e9, "near": 0.5e9, "row": 0.5e9, "late": 0.01e9,
-    "audio_sum": 5e9, "video_sum": 20e9, "row_sum": 0.5e9,
+    "audio_sum": 5e9, "imu_sum": 0.01e9, "col_sum": 20e9, "row_sum": 0.5e9,
 }
 
 F32 = jnp.float32
@@ -227,25 +227,21 @@
     return jnp.sum(packed[rows:, :rows].astype(F32), axis=0, keepdims=True)
 
 
-def audio_sum_kernel(got_audio, audio_in, loss_in, audio_grad, loss, buffer, done):
-    copies = added((audio_in, got_audio), audio_grad, buffer, done)
+def partner_sum_kernel(got, grad_in, loss_in, grad, loss, buffer, done):
+    copies = added((grad_in, got), grad, buffer, done)
     loss[...] = loss_in[...]
     for copy in copies:
         copy.wait()
 
 
-def video_sum_kernel(got_video, video_in, loss_in, video_grad, loss):
+def col_sum_kernel(got_video, video_in, loss_in, video_grad, loss):
     rows = video_grad.shape[0]
     video_grad[...] = video_in[...] + got_video[:rows, :].astype(F32)
     loss[...] = loss_in[...] + losses_in(got_video)
 
 
-def row_sum_kernel(
-    got_video, got_imu, video_in, imu_in, loss_in, video_grad, imu_grad, loss,
-    video_buffer, video_done, imu_buffer, imu_done,
-):
-    copies = added((video_in, got_video), video_grad, video_buffer, video_done)
-    copies += added((imu_in, got_imu), imu_grad, imu_buffer, imu_done)
+def row_sum_kernel(got_video, video_in, loss_in, video_grad, loss, buffer, done):
+    copies = added((video_in, got_video), video_grad, buffer, done)
     rows = video_in.shape[0]
     total = loss_in[...] + losses_in(got_video)
     loss[...] = (total / (2.0 * STEPS * rows)).reshape(rows)
@@ -380,24 +376,31 @@
 
     hbm, vmem = pltpu.HBM, pltpu.VMEM
     audio_grad, loss = summed(
-        audio_sum_kernel,
+        partner_sum_kernel,
         [square, line],
         [hbm, vmem],
         (got_audio, audio_grad, loss),
         COSTS["audio_sum"],
     )
+    imu_grad, loss = summed(
+        partner_sum_kernel,
+        [square, line],
+        [hbm, vmem],
+        (got_imu, imu_grad, loss),
+        COSTS["imu_sum"],
+    )
     video_grad, loss = summed(
-        video_sum_kernel,
+        col_sum_kernel,
         [square, line],
         [vmem, vmem],
         (got_col, video_grad, loss),
-        COSTS["video_sum"],
-    )
-    video_grad, imu_grad, loss = summed(
+        COSTS["col_sum"],
+    )
+    video_grad, loss = summed(
         row_sum_kernel,
-        [square, square, ((rows,), F32)],
-        [hbm, hbm, vmem],
-        (got_row, got_imu, video_grad, imu_grad, loss),
+        [square, ((rows,), F32)],
+        [hbm, vmem],
+        (got_row, video_grad, loss),
         COSTS["row_sum"],
     )
     return (video_grad, imu_grad, audio_grad, loss)

time: 84.9 us -> 84.3 us (level)
  waiting for transfers between devices: 48.6 us -> 47.3 us
    ppermute x2, waiting for transfers between devices: 1.4 us -> 0.18 us  [return_video(): return lax.ppermute(block, self.axis, [(b, a) for a, b in self.video])]
    pallas_call x3 -> x4, Pallas kernels: 3.69 us -> 4.34 us  [summed(): pl.pallas_call(kernel, out_shape=[jax.ShapeDtypeStruct(*out) for out in o...]
  transfers between devices with their start and end apart: 9 -> 9, of which waited for: 4 -> 4; matrix products, arithmetic and copies ran while one was open for 0% -> 0% of each run, Pallas kernels for 20% -> 22%
where the time goes in v2:
time: 84.3 us; the launch traced here: 84.2 us
  waiting for transfers between devices  47.3 us (56%)
  Pallas kernels  20 us (24%)
  starting transfers between devices  13.4 us (16%)
  between operations  3.34 us (4%)
    ppermute x3, waiting for transfers between devices, bring_partner(): return lax.ppermute(block, self.axis, self.partner)  23.3 us
    ppermute x2, waiting for transfers between devices, return_partner(): return lax.ppermute(block, self.axis, [(b, a) for a, b in self.partner])  22.7 us
    pallas_call x6, Pallas kernels, call(): pl.pallas_call(kernel, out_shape=[jax.ShapeDtypeStruct(*out) for out in o...  14.3 us
    ppermute x2, starting transfers between devices, return_partner(): return lax.ppermute(block, self.axis, [(b, a) for a, b in self.partner])  4.7 us
    ppermute x3, starting transfers between devices, bring_partner(): return lax.ppermute(block, self.axis, self.partner)  4.66 us
    pallas_call x4, Pallas kernels, summed(): pl.pallas_call(kernel, out_shape=[jax.ShapeDtypeStruct(*out) for out in o...  4.34 us
    ppermute x2, starting transfers between devices, bring_video(): return lax.ppermute(block, self.axis, self.video)  3.03 us
  transfers between devices with their start and end apart: 9, of which 4 were waited for; matrix products, arithmetic and copies ran while one was open for 0% of the time, Pallas kernels for 22%

profile of v2, /device:TPU:0, one launch (start us, length us, event | category | flops | bytes accessed | tf_op | source)
XLA Modules:
  0.0 84.2 jit_solution(9073239335888364206)
XLA Ops:
  0.6 0.0 copy-start
  0.6 0.0 copy-start.1
  0.7 4.1 %collective-permute-start.3 = (bf16[384,1024]{1,0:T(8,128)(2,1)}, bf16[384,1024]{1,0:T(8,128)(2,1)S(1)}, u32[]{:S(2)}, u32[]{:S(2)}) collective-permute-start(bf16[384,1024]{1,0:T(8,128)(2,1)} %audio.3), channel_id=1, source_target_pairs={{2,0},{3,1},{0,2},{1,3},{6,4},{7,5},{4,6},{5,7},{10,8},{11,9},{8,1... | collective-permute-start | bytes 2359304 | tf_op jit(solution)/shard_map/ppermute | solution.py:300
  4.8 1.4 %shard_map.129 = (bf16[400,1024]{1,0:T(8,128)(2,1)S(1)}, bf16[400,1024]{1,0:T(8,128)(2,1)S(1)}) custom-call(bf16[384,1024]{1,0:T(8,128)(2,1)} %refs_0_.1, bf16[384,1024]{1,0:T(8,128)(2,1)} %refs_1_.1, s32[384]{0:T(512)} %refs_2_.1, s32[384]{0:T(512)} %refs_3_.1), custom_call_target="tpu_custom_call" | custom-call | tf_op jit(solution)/shard_map/pallas_call | solution.py:52
  6.2 1.6 %collective-permute-start.2 = (bf16[400,1024]{1,0:T(8,128)(2,1)S(1)}, bf16[400,1024]{1,0:T(8,128)(2,1)S(1)}, u32[]{:S(2)}, u32[]{:S(2)}) collective-permute-start(bf16[400,1024]{1,0:T(8,128)(2,1)S(1)} %get-tuple-element.38.video), channel_id=1, source_target_pairs={{1,0},{0,1},{3,2},{2,3},{5,4},{4,5},{7,6},{6,7},{9,8},{8,9},{11,10... | collective-permute-start | bytes 2457608 | tf_op jit(solution)/shard_map/ppermute | solution.py:297
  10.4 0.0 copy-done
  10.4 0.0 copy-done.1
  10.5 3.8 %shard_map.130 = (f32[1,384]{1,0:T(1,128)S(1)}, f32[384,1024]{1,0:T(8,128)S(1)}, f32[384,1024]{1,0:T(8,128)S(1)}, f32[384,1024]{1,0:T(8,128)S(1)}, bf16[400,1024...) custom-call(f32[1]{0:T(128)S(6)} %copy.14.imu_log_scale.log_scale, f32[1]{0:T(128)S(6)} %copy.15.imu_bias.bias, ...), custom_call_target="tpu_custom_call" | custom-call | flops 500000000 | bytes 4852736 | tf_op jit(solution)/shard_map/pallas_call | solution.py:270
  14.2 1.4 %collective-permute-start = (bf16[400,1024]{1,0:T(8,128)(2,1)S(1)}, bf16[400,1024]{1,0:T(8,128)(2,1)S(1)}, u32[]{:S(2)}, u32[]{:S(2)}) collective-permute-start(bf16[400,1024]{1,0:T(8,128)(2,1)S(1)} %get-tuple-element.40), channel_id=1, source_target_pairs={{4,0},{8,4},{12,8},{16,12},{20,16},{24,20},{28,24},{0,28},{5,1},{9... | collective-permute-start | bytes 2457608 | tf_op jit(solution)/shard_map/ppermute | solution.py:297
  15.6 0.2 collective-permute-start.1
  15.8 0.3 collective-permute-start.4
  16.2 23.3 %collective-permute-done.4.audio_ids = s32[384]{0:T(512)S(1)} collective-permute-done((s32[384]{0:T(512)S(1)}, s32[384]{0:T(512)S(1)}, u32[]{:S(2)}, u32[]{:S(2)}) %collective-permute-start.4) | collective-permute-done | bytes 1568 | tf_op jit(solution)/shard_map/ppermute | solution.py:300
  39.5 0.0 collective-permute-done.3.audio.far_audio
  39.5 1.0 %shard_map.131 = (f32[1,384]{1,0:T(1,128)S(1)}, bf16[384,384]{1,0:T(8,128)(2,1)S(1)}) custom-call(f32[1]{0:T(128)S(6)} %copy.16.audio_log_scale.log_scale, f32[1]{0:T(128)S(6)} %copy.17.audio_bias.bias, bf16[400,1024]{1,0:T(8,128)(2,1)S(1)} %get-tuple-element.38.video, bf16[384,1024]{1,0:T(8,128)(2,1)S(1)} %collective-permute-done.3.audio.far_audio, ...), custom_call_target="tpu_custom_call" | custom-call | flops 500000000 | bytes 3217408 | tf_op jit(solution)/shard_map/pallas_call | solution.py:270
  40.5 1.2 %collective-permute-done.2.other_video.col_video = bf16[400,1024]{1,0:T(8,128)(2,1)S(1)} collective-permute-done((bf16[400,1024]{1,0:T(8,128)(2,1)S(1)}, bf16[400,1024]{1,0:T(8,128)(2,1)S(1)}, u32[]{:S(2)}, u32[]{:S(2)}) %collective-permute-start.2) | collective-permute-done | bytes 819232 | tf_op jit(solution)/shard_map/ppermute | solution.py:297
  41.7 1.9 %shard_map.132 = (f32[1,384]{1,0:T(1,128)S(1)}, f32[1,384]{1,0:T(1,128)S(1)}, bf16[384,1024]{1,0:T(8,128)(2,1)S(1)}, bf16[384,384]{1,0:T(8,128)(2,1)S(1)}) custom-call(f32[1]{0:T(128)S(6)} %copy.16.audio_log_scale.log_scale, f32[1]{0:T(128)S(6)} %copy.17.audio_bias.bias, bf16[400,1024]{1,0:T(8,128)(2,1)S(1)} %get-tuple-element.38.video, ...), custom_call_target="tpu_custom_call" | custom-call | flops 500000000 | bytes 5445632 | tf_op jit(solution)/shard_map/pallas_call | solution.py:270
  43.6 2.2 %collective-permute-start.8 = (bf16[384,1024]{1,0:T(8,128)(2,1)S(1)}, bf16[384,1024]{1,0:T(8,128)(2,1)S(1)}, u32[]{:S(2)}, u32[]{:S(2)}) collective-permute-start(bf16[384,1024]{1,0:T(8,128)(2,1)S(1)} %get-tuple-element.61), channel_id=1, source_target_pairs={{0,2},{1,3},{2,0},{3,1},{4,6},{5,7},{6,4},{7,5},{8,10},{9,11},{10,... | collective-permute-start | bytes 2359304 | tf_op jit(solution)/shard_map/ppermute | solution.py:306
  45.8 1.8 %shard_map.133 = (bf16[400,1024]{1,0:T(8,128)(2,1)S(1)}, bf16[384,384]{1,0:T(8,128)(2,1)S(1)}, f32[1,384]{1,0:T(1,128)S(1)}) custom-call(f32[1]{0:T(128)S(6)} %copy.16.audio_log_scale.log_scale, f32[1]{0:T(128)S(6)} %copy.17.audio_bias.bias, bf16[400,1024]{1,0:T(8,128)(2,1)S(1)} %collective-permute-done.2.other_video.col_video, ...), custom_call_target="tpu_custom_call" | custom-call | flops 500000000 | bytes 5383168 | tf_op jit(solution)/shard_map/pallas_call | solution.py:270
  47.6 1.0 %collective-permute-start.6 = (bf16[400,1024]{1,0:T(8,128)(2,1)S(1)}, bf16[400,1024]{1,0:T(8,128)(2,1)S(1)}, u32[]{:S(2)}, u32[]{:S(2)}) collective-permute-start(bf16[400,1024]{1,0:T(8,128)(2,1)S(1)} %get-tuple-element.50), channel_id=1, source_target_pairs={{0,1},{1,0},{2,3},{3,2},{4,5},{5,4},{6,7},{7,6},{8,9},{9,8},{10,11... | collective-permute-start | bytes 2457608 | tf_op jit(solution)/shard_map/ppermute | solution.py:303
  48.6 0.0 collective-permute-done.other_video.row_video
  48.6 0.0 collective-permute-done.1.other_imu.row_imu
  48.6 4.0 %shard_map.134 = (f32[1,384]{1,0:T(1,128)S(1)}, bf16[400,1024]{1,0:T(8,128)(2,1)S(1)}, bf16[384,1024]{1,0:T(8,128)(2,1)S(1)}, bf16[384,384]{1,0:T(8,128)(2,1)S(1)}, bf16[384,384]{1,0:T(8,128)(2,1)S(1)}) custom-call(f32[1]{0:T(128)S(6)} %copy.14.imu_log_scale.log_scale, f32[1]{0:T(128)S(6)} %copy.15.imu_bias.bias, ...), custom_call_target="tpu_custom_call" | custom-call | flops 500000000 | bytes 6556672 | tf_op jit(solution)/shard_map/pallas_call | solution.py:270
  52.6 2.5 %collective-permute-start.7 = (bf16[384,1024]{1,0:T(8,128)(2,1)S(1)}, bf16[384,1024]{1,0:T(8,128)(2,1)S(1)}, u32[]{:S(2)}, u32[]{:S(2)}) collective-permute-start(bf16[384,1024]{1,0:T(8,128)(2,1)S(1)} %get-tuple-element.59), channel_id=1, source_target_pairs={{0,24},{4,28},{8,0},{12,4},{16,8},{20,12},{24,16},{28,20},{1,25},{... | collective-permute-start | bytes 2359304 | tf_op jit(solution)/shard_map/ppermute | solution.py:306
  55.1 0.0 collective-permute-start.5
  55.1 1.9 %shard_map.135 = (f32[384,1024]{1,0:T(8,128)S(1)}, f32[384,1024]{1,0:T(8,128)S(1)}, f32[384,1024]{1,0:T(8,128)S(1)}, f32[1,384]{1,0:T(1,128)S(1)}) custom-call(bf16[384,1024]{1,0:T(8,128)(2,1)S(1)} %collective-permute-done.3.audio.far_audio, bf16[384,384]{1,0:T(8,128)(2,1)S(1)} %get-tuple-element.43.own_weights.far_weights, ...), custom_call_target="tpu_custom_call" | custom-call | flops 10000000 | bytes 18287616 | tf_op jit(solution)/shard_map/pallas_call | solution.py:270
  56.9 22.7 %collective-permute-done.8.got = bf16[384,1024]{1,0:T(8,128)(2,1)S(1)} collective-permute-done((bf16[384,1024]{1,0:T(8,128)(2,1)S(1)}, bf16[384,1024]{1,0:T(8,128)(2,1)S(1)}, u32[]{:S(2)}, u32[]{:S(2)}) %collective-permute-start.8) | collective-permute-done | bytes 786464 | tf_op jit(solution)/shard_map/ppermute | solution.py:306
  79.6 1.2 %shard_map.136 = (f32[384,1024]{1,0:T(8,128)}, f32[1,384]{1,0:T(1,128)S(1)}) custom-call(bf16[384,1024]{1,0:T(8,128)(2,1)S(1)} %collective-permute-done.8.got, f32[384,1024]{1,0:T(8,128)S(1)} %get-tuple-element.62.grad_in, f32[1,384]{1,0:T(1,128)S(1)} %get-tuple-element.63.loss_in), custom_call_target="tpu_custom_call" | custom-call | flops 5000000000 | tf_op jit(solution)/shard_map/pallas_call | solution.py:254
  80.8 0.0 collective-permute-done.7.got
  80.8 1.2 %shard_map.137 = (f32[384,1024]{1,0:T(8,128)}, f32[1,384]{1,0:T(1,128)S(1)}) custom-call(bf16[384,1024]{1,0:T(8,128)(2,1)S(1)} %collective-permute-done.7.got, f32[384,1024]{1,0:T(8,128)S(1)} %get-tuple-element.60.grad_in, f32[1,384]{1,0:T(1,128)S(1)} %get-tuple-element.64.loss_in), custom_call_target="tpu_custom_call" | custom-call | flops 10000000 | tf_op jit(solution)/shard_map/pallas_call | solution.py:254
  82.1 0.2 collective-permute-done.6.got_video
  82.2 0.1 shard_map.138
  82.4 0.0 collective-permute-done.5.got_video
  82.4 1.8 %shard_map.139 = (f32[384,1024]{1,0:T(8,128)}, f32[384]{0:T(512)}) custom-call(bf16[400,1024]{1,0:T(8,128)(2,1)S(1)} %collective-permute-done.5.got_video, f32[384,1024]{1,0:T(8,128)S(1)} %get-tuple-element.66.video_in, f32[1,384]{1,0:T(1,128)S(1)} %get-tuple-element.67.loss_in), custom_call_target="tpu_custom_call" | custom-call | flops 500000000 | tf_op jit(solution)/shard_map/pallas_call | solution.py:254
Async XLA Ops:
  0.6 9.8 %copy-start = (bf16[384,1024]{1,0:T(8,128)(2,1)S(1)}, bf16[384,1024]{1,0:T(8,128)(2,1)}, u32[]{:S(2)}) copy-start(bf16[384,1024]{1,0:T(8,128)(2,1)} %audio.3) | copy-start | bytes 2359300
  0.6 9.8 %copy-start.1 = (s32[384]{0:T(512)S(1)}, s32[384]{0:T(512)}, u32[]{:S(2)}) copy-start(s32[384]{0:T(512)} %audio_ids.3) | copy-start | bytes 4612
  0.7 38.9 %collective-permute-start.3 = (bf16[384,1024]{1,0:T(8,128)(2,1)}, bf16[384,1024]{1,0:T(8,128)(2,1)S(1)}, u32[]{:S(2)}, u32[]{:S(2)}) collective-permute-start(bf16[384,1024]{1,0:T(8,128)(2,1)} %audio.3), channel_id=1, source_target_pairs={{2,0},{3,1},{0,2},{1,3},{6,4},{7,5},{4,6},{5,7},{10,8},{11,9},{8,1... | collective-permute-start | bytes 2359304 | tf_op jit(solution)/shard_map/ppermute | solution.py:300
  6.2 35.5 %collective-permute-start.2 = (bf16[400,1024]{1,0:T(8,128)(2,1)S(1)}, bf16[400,1024]{1,0:T(8,128)(2,1)S(1)}, u32[]{:S(2)}, u32[]{:S(2)}) collective-permute-start(bf16[400,1024]{1,0:T(8,128)(2,1)S(1)} %get-tuple-element.38.video), channel_id=1, source_target_pairs={{1,0},{0,1},{3,2},{2,3},{5,4},{4,5},{7,6},{6,7},{9,8},{8,9},{11,10... | collective-permute-start | bytes 2457608 | tf_op jit(solution)/shard_map/ppermute | solution.py:297
  14.2 34.4 %collective-permute-start = (bf16[400,1024]{1,0:T(8,128)(2,1)S(1)}, bf16[400,1024]{1,0:T(8,128)(2,1)S(1)}, u32[]{:S(2)}, u32[]{:S(2)}) collective-permute-start(bf16[400,1024]{1,0:T(8,128)(2,1)S(1)} %get-tuple-element.40), channel_id=1, source_target_pairs={{4,0},{8,4},{12,8},{16,12},{20,16},{24,20},{28,24},{0,28},{5,1},{9... | collective-permute-start | bytes 2457608 | tf_op jit(solution)/shard_map/ppermute | solution.py:297
  15.6 33.0 %collective-permute-start.1 = (bf16[400,1024]{1,0:T(8,128)(2,1)S(1)}, bf16[400,1024]{1,0:T(8,128)(2,1)S(1)}, u32[]{:S(2)}, u32[]{:S(2)}) collective-permute-start(bf16[400,1024]{1,0:T(8,128)(2,1)S(1)} %get-tuple-element.41), channel_id=1, source_target_pairs={{24,0},{28,4},{0,8},{4,12},{8,16},{12,20},{16,24},{20,28},{25,1},{... | collective-permute-start | bytes 2457608 | tf_op jit(solution)/shard_map/ppermute | solution.py:300
  15.8 23.7 %collective-permute-start.4 = (s32[384]{0:T(512)S(1)}, s32[384]{0:T(512)S(1)}, u32[]{:S(2)}, u32[]{:S(2)}) collective-permute-start(s32[384]{0:T(512)S(1)} %copy-done.1), channel_id=1, source_target_pairs={{2,0},{3,1},{0,2},{1,3},{6,4},{7,5},{4,6},{5,7},{10,8},{11,9},{8,1... | collective-permute-start | bytes 4616 | tf_op jit(solution)/shard_map/ppermute | solution.py:300
  43.6 36.0 %collective-permute-start.8 = (bf16[384,1024]{1,0:T(8,128)(2,1)S(1)}, bf16[384,1024]{1,0:T(8,128)(2,1)S(1)}, u32[]{:S(2)}, u32[]{:S(2)}) collective-permute-start(bf16[384,1024]{1,0:T(8,128)(2,1)S(1)} %get-tuple-element.61), channel_id=1, source_target_pairs={{0,2},{1,3},{2,0},{3,1},{4,6},{5,7},{6,4},{7,5},{8,10},{9,11},{10,... | collective-permute-start | bytes 2359304 | tf_op jit(solution)/shard_map/ppermute | solution.py:306
  47.6 34.7 %collective-permute-start.6 = (bf16[400,1024]{1,0:T(8,128)(2,1)S(1)}, bf16[400,1024]{1,0:T(8,128)(2,1)S(1)}, u32[]{:S(2)}, u32[]{:S(2)}) collective-permute-start(bf16[400,1024]{1,0:T(8,128)(2,1)S(1)} %get-tuple-element.50), channel_id=1, source_target_pairs={{0,1},{1,0},{2,3},{3,2},{4,5},{5,4},{6,7},{7,6},{8,9},{9,8},{10,11... | collective-permute-start | bytes 2457608 | tf_op jit(solution)/shard_map/ppermute | solution.py:303
  52.6 28.3 %collective-permute-start.7 = (bf16[384,1024]{1,0:T(8,128)(2,1)S(1)}, bf16[384,1024]{1,0:T(8,128)(2,1)S(1)}, u32[]{:S(2)}, u32[]{:S(2)}) collective-permute-start(bf16[384,1024]{1,0:T(8,128)(2,1)S(1)} %get-tuple-element.59), channel_id=1, source_target_pairs={{0,24},{4,28},{8,0},{12,4},{16,8},{20,12},{24,16},{28,20},{1,25},{... | collective-permute-start | bytes 2359304 | tf_op jit(solution)/shard_map/ppermute | solution.py:306
  55.1 27.3 %collective-permute-start.5 = (bf16[400,1024]{1,0:T(8,128)(2,1)S(1)}, bf16[400,1024]{1,0:T(8,128)(2,1)S(1)}, u32[]{:S(2)}, u32[]{:S(2)}) collective-permute-start(bf16[400,1024]{1,0:T(8,128)(2,1)S(1)} %get-tuple-element.49), channel_id=1, source_target_pairs={{0,4},{4,8},{8,12},{12,16},{16,20},{20,24},{24,28},{28,0},{1,5},{5... | collective-permute-start | bytes 2457608 | tf_op jit(solution)/shard_map/ppermute | solution.py:303

commit v3 on v2

--- a/solution.py
+++ b/solution.py
@@ -240,13 +240,17 @@
     loss[...] = loss_in[...] + losses_in(got_video)
 
 
-def row_sum_kernel(got_video, video_in, loss_in, video_grad, loss, buffer, done):
-    copies = added((video_in, got_video), video_grad, buffer, done)
+def row_sum_kernel(
+    got_video, video_in, loss_in, video_grad, loss, buffer, done, losses, losses_done
+):
     rows = video_in.shape[0]
     total = loss_in[...] + losses_in(got_video)
-    loss[...] = (total / (2.0 * STEPS * rows)).reshape(rows)
-    for copy in copies:
-        copy.wait()
+    losses[...] = (total / (2.0 * STEPS * rows)).reshape(rows)
+    copy = pltpu.make_async_copy(losses, loss, losses_done)
+    copy.start()
+    for part in added((video_in, got_video), video_grad, buffer, done):
+        part.wait()
+    copy.wait()
 
 
 def summed(kernel, outs, spaces, args, cost):
@@ -256,8 +260,15 @@
         out_shape=[jax.ShapeDtypeStruct(*out) for out in outs],
         in_specs=[vmem] * len(args),
         out_specs=[pl.BlockSpec(memory_space=space) for space in spaces],
-        scratch_shapes=[pltpu.VMEM(outs[0][0], F32), pltpu.SemaphoreType.DMA((SUM_BLOCKS,))]
-        * sum(space == pltpu.HBM for space in spaces),
+        scratch_shapes=[
+            scratch
+            for (shape, _), space in zip(outs, spaces)
+            if space == pltpu.HBM
+            for scratch in (
+                pltpu.VMEM(shape, F32),
+                pltpu.SemaphoreType.DMA((SUM_BLOCKS,) if len(shape) == 2 else ()),
+            )
+        ],
         compiler_params=pltpu.CompilerParams(vmem_limit_bytes=20 * 2**20),
         cost_estimate=pl.CostEstimate(flops=int(cost), bytes_accessed=0, transcendentals=0),
     )(*args)
@@ -399,7 +410,7 @@
     video_grad, loss = summed(
         row_sum_kernel,
         [square, ((rows,), F32)],
-        [hbm, vmem],
+        [hbm, hbm],
         (got_row, video_grad, loss),
         COSTS["row_sum"],
     )

time: 84.3 us -> 83.8 us (level)
  no operation moved by 1% of the time
where the time goes in v3:
time: 83.8 us; the launch traced here: 83.6 us
  waiting for transfers between devices  47.3 us (56%)
  Pallas kernels  19.5 us (23%)
  starting transfers between devices  13.4 us (16%)
  between operations  3.34 us (4%)
    ppermute x3, waiting for transfers between devices, bring_partner(): return lax.ppermute(block, self.axis, self.partner)  23.3 us
    ppermute x2, waiting for transfers between devices, return_partner(): return lax.ppermute(block, self.axis, [(b, a) for a, b in self.partner])  22.7 us
    pallas_call x6, Pallas kernels, call(): pl.pallas_call(kernel, out_shape=[jax.ShapeDtypeStruct(*out) for out in o...  14.3 us
    ppermute x2, starting transfers between devices, return_partner(): return lax.ppermute(block, self.axis, [(b, a) for a, b in self.partner])  4.7 us
    ppermute x3, starting transfers between devices, bring_partner(): return lax.ppermute(block, self.axis, self.partner)  4.66 us
    pallas_call x4, Pallas kernels, summed(): pl.pallas_call(kernel, out_shape=[jax.ShapeDtypeStruct(*out) for out in o...  3.8 us
    ppermute x2, starting transfers between devices, bring_video(): return lax.ppermute(block, self.axis, self.video)  3.03 us
  transfers between devices with their start and end apart: 9, of which 4 were waited for; matrix products, arithmetic and copies ran while one was open for 0% of the time, Pallas kernels for 22%

profile of v3, /device:TPU:0, one launch (start us, length us, event | category | flops | bytes accessed | tf_op | source)
XLA Modules:
  0.0 83.6 jit_solution(12231368173693550051)
XLA Ops:
  0.6 0.0 copy-start
  0.6 0.0 copy-start.1
  0.7 4.1 %collective-permute-start.3 = (bf16[384,1024]{1,0:T(8,128)(2,1)}, bf16[384,1024]{1,0:T(8,128)(2,1)S(1)}, u32[]{:S(2)}, u32[]{:S(2)}) collective-permute-start(bf16[384,1024]{1,0:T(8,128)(2,1)} %audio.3), channel_id=1, source_target_pairs={{2,0},{3,1},{0,2},{1,3},{6,4},{7,5},{4,6},{5,7},{10,8},{11,9},{8,1... | collective-permute-start | bytes 2359304 | tf_op jit(solution)/shard_map/ppermute | solution.py:311
  4.8 1.4 %shard_map.129 = (bf16[400,1024]{1,0:T(8,128)(2,1)S(1)}, bf16[400,1024]{1,0:T(8,128)(2,1)S(1)}) custom-call(bf16[384,1024]{1,0:T(8,128)(2,1)} %refs_0_.1, bf16[384,1024]{1,0:T(8,128)(2,1)} %refs_1_.1, s32[384]{0:T(512)} %refs_2_.1, s32[384]{0:T(512)} %refs_3_.1), custom_call_target="tpu_custom_call" | custom-call | tf_op jit(solution)/shard_map/pallas_call | solution.py:52
  6.2 1.6 %collective-permute-start.2 = (bf16[400,1024]{1,0:T(8,128)(2,1)S(1)}, bf16[400,1024]{1,0:T(8,128)(2,1)S(1)}, u32[]{:S(2)}, u32[]{:S(2)}) collective-permute-start(bf16[400,1024]{1,0:T(8,128)(2,1)S(1)} %get-tuple-element.38.video), channel_id=1, source_target_pairs={{1,0},{0,1},{3,2},{2,3},{5,4},{4,5},{7,6},{6,7},{9,8},{8,9},{11,10... | collective-permute-start | bytes 2457608 | tf_op jit(solution)/shard_map/ppermute | solution.py:308
  10.4 0.0 copy-done
  10.4 0.0 copy-done.1
  10.5 3.8 %shard_map.130 = (f32[1,384]{1,0:T(1,128)S(1)}, f32[384,1024]{1,0:T(8,128)S(1)}, f32[384,1024]{1,0:T(8,128)S(1)}, f32[384,1024]{1,0:T(8,128)S(1)}, bf16[400,1024...) custom-call(f32[1]{0:T(128)S(6)} %copy.14.imu_log_scale.log_scale, f32[1]{0:T(128)S(6)} %copy.15.imu_bias.bias, ...), custom_call_target="tpu_custom_call" | custom-call | flops 500000000 | bytes 4852736 | tf_op jit(solution)/shard_map/pallas_call | solution.py:281
  14.2 1.4 %collective-permute-start = (bf16[400,1024]{1,0:T(8,128)(2,1)S(1)}, bf16[400,1024]{1,0:T(8,128)(2,1)S(1)}, u32[]{:S(2)}, u32[]{:S(2)}) collective-permute-start(bf16[400,1024]{1,0:T(8,128)(2,1)S(1)} %get-tuple-element.40), channel_id=1, source_target_pairs={{4,0},{8,4},{12,8},{16,12},{20,16},{24,20},{28,24},{0,28},{5,1},{9... | collective-permute-start | bytes 2457608 | tf_op jit(solution)/shard_map/ppermute | solution.py:308
  15.6 0.2 collective-permute-start.1
  15.8 0.3 collective-permute-start.4
  16.2 23.3 %collective-permute-done.4.audio_ids = s32[384]{0:T(512)S(1)} collective-permute-done((s32[384]{0:T(512)S(1)}, s32[384]{0:T(512)S(1)}, u32[]{:S(2)}, u32[]{:S(2)}) %collective-permute-start.4) | collective-permute-done | bytes 1568 | tf_op jit(solution)/shard_map/ppermute | solution.py:311
  39.5 0.0 collective-permute-done.3.audio.far_audio
  39.5 1.0 %shard_map.131 = (f32[1,384]{1,0:T(1,128)S(1)}, bf16[384,384]{1,0:T(8,128)(2,1)S(1)}) custom-call(f32[1]{0:T(128)S(6)} %copy.16.audio_log_scale.log_scale, f32[1]{0:T(128)S(6)} %copy.17.audio_bias.bias, bf16[400,1024]{1,0:T(8,128)(2,1)S(1)} %get-tuple-element.38.video, bf16[384,1024]{1,0:T(8,128)(2,1)S(1)} %collective-permute-done.3.audio.far_audio, ...), custom_call_target="tpu_custom_call" | custom-call | flops 500000000 | bytes 3217408 | tf_op jit(solution)/shard_map/pallas_call | solution.py:281
  40.5 1.2 %collective-permute-done.2.other_video.col_video = bf16[400,1024]{1,0:T(8,128)(2,1)S(1)} collective-permute-done((bf16[400,1024]{1,0:T(8,128)(2,1)S(1)}, bf16[400,1024]{1,0:T(8,128)(2,1)S(1)}, u32[]{:S(2)}, u32[]{:S(2)}) %collective-permute-start.2) | collective-permute-done | bytes 819232 | tf_op jit(solution)/shard_map/ppermute | solution.py:308
  41.7 1.9 %shard_map.132 = (f32[1,384]{1,0:T(1,128)S(1)}, f32[1,384]{1,0:T(1,128)S(1)}, bf16[384,1024]{1,0:T(8,128)(2,1)S(1)}, bf16[384,384]{1,0:T(8,128)(2,1)S(1)}) custom-call(f32[1]{0:T(128)S(6)} %copy.16.audio_log_scale.log_scale, f32[1]{0:T(128)S(6)} %copy.17.audio_bias.bias, bf16[400,1024]{1,0:T(8,128)(2,1)S(1)} %get-tuple-element.38.video, ...), custom_call_target="tpu_custom_call" | custom-call | flops 500000000 | bytes 5445632 | tf_op jit(solution)/shard_map/pallas_call | solution.py:281
  43.6 2.2 %collective-permute-start.8 = (bf16[384,1024]{1,0:T(8,128)(2,1)S(1)}, bf16[384,1024]{1,0:T(8,128)(2,1)S(1)}, u32[]{:S(2)}, u32[]{:S(2)}) collective-permute-start(bf16[384,1024]{1,0:T(8,128)(2,1)S(1)} %get-tuple-element.61), channel_id=1, source_target_pairs={{0,2},{1,3},{2,0},{3,1},{4,6},{5,7},{6,4},{7,5},{8,10},{9,11},{10,... | collective-permute-start | bytes 2359304 | tf_op jit(solution)/shard_map/ppermute | solution.py:317
  45.8 1.8 %shard_map.133 = (bf16[400,1024]{1,0:T(8,128)(2,1)S(1)}, bf16[384,384]{1,0:T(8,128)(2,1)S(1)}, f32[1,384]{1,0:T(1,128)S(1)}) custom-call(f32[1]{0:T(128)S(6)} %copy.16.audio_log_scale.log_scale, f32[1]{0:T(128)S(6)} %copy.17.audio_bias.bias, bf16[400,1024]{1,0:T(8,128)(2,1)S(1)} %collective-permute-done.2.other_video.col_video, ...), custom_call_target="tpu_custom_call" | custom-call | flops 500000000 | bytes 5383168 | tf_op jit(solution)/shard_map/pallas_call | solution.py:281
  47.6 1.0 %collective-permute-start.6 = (bf16[400,1024]{1,0:T(8,128)(2,1)S(1)}, bf16[400,1024]{1,0:T(8,128)(2,1)S(1)}, u32[]{:S(2)}, u32[]{:S(2)}) collective-permute-start(bf16[400,1024]{1,0:T(8,128)(2,1)S(1)} %get-tuple-element.50), channel_id=1, source_target_pairs={{0,1},{1,0},{2,3},{3,2},{4,5},{5,4},{6,7},{7,6},{8,9},{9,8},{10,11... | collective-permute-start | bytes 2457608 | tf_op jit(solution)/shard_map/ppermute | solution.py:314
  48.6 0.0 collective-permute-done.other_video.row_video
  48.6 0.0 collective-permute-done.1.other_imu.row_imu
  48.6 4.0 %shard_map.134 = (f32[1,384]{1,0:T(1,128)S(1)}, bf16[400,1024]{1,0:T(8,128)(2,1)S(1)}, bf16[384,1024]{1,0:T(8,128)(2,1)S(1)}, bf16[384,384]{1,0:T(8,128)(2,1)S(1)}, bf16[384,384]{1,0:T(8,128)(2,1)S(1)}) custom-call(f32[1]{0:T(128)S(6)} %copy.14.imu_log_scale.log_scale, f32[1]{0:T(128)S(6)} %copy.15.imu_bias.bias, ...), custom_call_target="tpu_custom_call" | custom-call | flops 500000000 | bytes 6556672 | tf_op jit(solution)/shard_map/pallas_call | solution.py:281
  52.6 2.5 %collective-permute-start.7 = (bf16[384,1024]{1,0:T(8,128)(2,1)S(1)}, bf16[384,1024]{1,0:T(8,128)(2,1)S(1)}, u32[]{:S(2)}, u32[]{:S(2)}) collective-permute-start(bf16[384,1024]{1,0:T(8,128)(2,1)S(1)} %get-tuple-element.59), channel_id=1, source_target_pairs={{0,24},{4,28},{8,0},{12,4},{16,8},{20,12},{24,16},{28,20},{1,25},{... | collective-permute-start | bytes 2359304 | tf_op jit(solution)/shard_map/ppermute | solution.py:317
  55.1 0.0 collective-permute-start.5
  55.1 1.9 %shard_map.135 = (f32[384,1024]{1,0:T(8,128)S(1)}, f32[384,1024]{1,0:T(8,128)S(1)}, f32[384,1024]{1,0:T(8,128)S(1)}, f32[1,384]{1,0:T(1,128)S(1)}) custom-call(bf16[384,1024]{1,0:T(8,128)(2,1)S(1)} %collective-permute-done.3.audio.far_audio, bf16[384,384]{1,0:T(8,128)(2,1)S(1)} %get-tuple-element.43.own_weights.far_weights, ...), custom_call_target="tpu_custom_call" | custom-call | flops 10000000 | bytes 18287616 | tf_op jit(solution)/shard_map/pallas_call | solution.py:281
  56.9 22.7 %collective-permute-done.8.got = bf16[384,1024]{1,0:T(8,128)(2,1)S(1)} collective-permute-done((bf16[384,1024]{1,0:T(8,128)(2,1)S(1)}, bf16[384,1024]{1,0:T(8,128)(2,1)S(1)}, u32[]{:S(2)}, u32[]{:S(2)}) %collective-permute-start.8) | collective-permute-done | bytes 786464 | tf_op jit(solution)/shard_map/ppermute | solution.py:317
  79.6 1.2 %shard_map.136 = (f32[384,1024]{1,0:T(8,128)}, f32[1,384]{1,0:T(1,128)S(1)}) custom-call(bf16[384,1024]{1,0:T(8,128)(2,1)S(1)} %collective-permute-done.8.got, f32[384,1024]{1,0:T(8,128)S(1)} %get-tuple-element.62.grad_in, f32[1,384]{1,0:T(1,128)S(1)} %get-tuple-element.63.loss_in), custom_call_target="tpu_custom_call" | custom-call | flops 5000000000 | tf_op jit(solution)/shard_map/pallas_call | solution.py:258
  80.8 0.0 collective-permute-done.7.got
  80.8 1.2 %shard_map.137 = (f32[384,1024]{1,0:T(8,128)}, f32[1,384]{1,0:T(1,128)S(1)}) custom-call(bf16[384,1024]{1,0:T(8,128)(2,1)S(1)} %collective-permute-done.7.got, f32[384,1024]{1,0:T(8,128)S(1)} %get-tuple-element.60.grad_in, f32[1,384]{1,0:T(1,128)S(1)} %get-tuple-element.64.loss_in), custom_call_target="tpu_custom_call" | custom-call | flops 10000000 | tf_op jit(solution)/shard_map/pallas_call | solution.py:258
  82.1 0.2 collective-permute-done.6.got_video
  82.2 0.1 shard_map.138
  82.4 0.0 collective-permute-done.5.got_video
  82.4 1.2 %shard_map.139 = (f32[384,1024]{1,0:T(8,128)}, f32[384]{0:T(512)}) custom-call(bf16[400,1024]{1,0:T(8,128)(2,1)S(1)} %collective-permute-done.5.got_video, f32[384,1024]{1,0:T(8,128)S(1)} %get-tuple-element.66.video_in, f32[1,384]{1,0:T(1,128)S(1)} %get-tuple-element.67.loss_in), custom_call_target="tpu_custom_call" | custom-call | flops 500000000 | tf_op jit(solution)/shard_map/pallas_call | solution.py:258
Async XLA Ops:
  0.6 9.8 %copy-start = (bf16[384,1024]{1,0:T(8,128)(2,1)S(1)}, bf16[384,1024]{1,0:T(8,128)(2,1)}, u32[]{:S(2)}) copy-start(bf16[384,1024]{1,0:T(8,128)(2,1)} %audio.3) | copy-start | bytes 2359300
  0.6 9.8 %copy-start.1 = (s32[384]{0:T(512)S(1)}, s32[384]{0:T(512)}, u32[]{:S(2)}) copy-start(s32[384]{0:T(512)} %audio_ids.3) | copy-start | bytes 4612
  0.7 38.9 %collective-permute-start.3 = (bf16[384,1024]{1,0:T(8,128)(2,1)}, bf16[384,1024]{1,0:T(8,128)(2,1)S(1)}, u32[]{:S(2)}, u32[]{:S(2)}) collective-permute-start(bf16[384,1024]{1,0:T(8,128)(2,1)} %audio.3), channel_id=1, source_target_pairs={{2,0},{3,1},{0,2},{1,3},{6,4},{7,5},{4,6},{5,7},{10,8},{11,9},{8,1... | collective-permute-start | bytes 2359304 | tf_op jit(solution)/shard_map/ppermute | solution.py:311
  6.2 35.5 %collective-permute-start.2 = (bf16[400,1024]{1,0:T(8,128)(2,1)S(1)}, bf16[400,1024]{1,0:T(8,128)(2,1)S(1)}, u32[]{:S(2)}, u32[]{:S(2)}) collective-permute-start(bf16[400,1024]{1,0:T(8,128)(2,1)S(1)} %get-tuple-element.38.video), channel_id=1, source_target_pairs={{1,0},{0,1},{3,2},{2,3},{5,4},{4,5},{7,6},{6,7},{9,8},{8,9},{11,10... | collective-permute-start | bytes 2457608 | tf_op jit(solution)/shard_map/ppermute | solution.py:308
  14.2 34.4 %collective-permute-start = (bf16[400,1024]{1,0:T(8,128)(2,1)S(1)}, bf16[400,1024]{1,0:T(8,128)(2,1)S(1)}, u32[]{:S(2)}, u32[]{:S(2)}) collective-permute-start(bf16[400,1024]{1,0:T(8,128)(2,1)S(1)} %get-tuple-element.40), channel_id=1, source_target_pairs={{4,0},{8,4},{12,8},{16,12},{20,16},{24,20},{28,24},{0,28},{5,1},{9... | collective-permute-start | bytes 2457608 | tf_op jit(solution)/shard_map/ppermute | solution.py:308
  15.6 33.0 %collective-permute-start.1 = (bf16[400,1024]{1,0:T(8,128)(2,1)S(1)}, bf16[400,1024]{1,0:T(8,128)(2,1)S(1)}, u32[]{:S(2)}, u32[]{:S(2)}) collective-permute-start(bf16[400,1024]{1,0:T(8,128)(2,1)S(1)} %get-tuple-element.41), channel_id=1, source_target_pairs={{24,0},{28,4},{0,8},{4,12},{8,16},{12,20},{16,24},{20,28},{25,1},{... | collective-permute-start | bytes 2457608 | tf_op jit(solution)/shard_map/ppermute | solution.py:311
  15.8 23.7 %collective-permute-start.4 = (s32[384]{0:T(512)S(1)}, s32[384]{0:T(512)S(1)}, u32[]{:S(2)}, u32[]{:S(2)}) collective-permute-start(s32[384]{0:T(512)S(1)} %copy-done.1), channel_id=1, source_target_pairs={{2,0},{3,1},{0,2},{1,3},{6,4},{7,5},{4,6},{5,7},{10,8},{11,9},{8,1... | collective-permute-start | bytes 4616 | tf_op jit(solution)/shard_map/ppermute | solution.py:311
  43.6 36.0 %collective-permute-start.8 = (bf16[384,1024]{1,0:T(8,128)(2,1)S(1)}, bf16[384,1024]{1,0:T(8,128)(2,1)S(1)}, u32[]{:S(2)}, u32[]{:S(2)}) collective-permute-start(bf16[384,1024]{1,0:T(8,128)(2,1)S(1)} %get-tuple-element.61), channel_id=1, source_target_pairs={{0,2},{1,3},{2,0},{3,1},{4,6},{5,7},{6,4},{7,5},{8,10},{9,11},{10,... | collective-permute-start | bytes 2359304 | tf_op jit(solution)/shard_map/ppermute | solution.py:317
  47.6 34.7 %collective-permute-start.6 = (bf16[400,1024]{1,0:T(8,128)(2,1)S(1)}, bf16[400,1024]{1,0:T(8,128)(2,1)S(1)}, u32[]{:S(2)}, u32[]{:S(2)}) collective-permute-start(bf16[400,1024]{1,0:T(8,128)(2,1)S(1)} %get-tuple-element.50), channel_id=1, source_target_pairs={{0,1},{1,0},{2,3},{3,2},{4,5},{5,4},{6,7},{7,6},{8,9},{9,8},{10,11... | collective-permute-start | bytes 2457608 | tf_op jit(solution)/shard_map/ppermute | solution.py:314
  52.6 28.3 %collective-permute-start.7 = (bf16[384,1024]{1,0:T(8,128)(2,1)S(1)}, bf16[384,1024]{1,0:T(8,128)(2,1)S(1)}, u32[]{:S(2)}, u32[]{:S(2)}) collective-permute-start(bf16[384,1024]{1,0:T(8,128)(2,1)S(1)} %get-tuple-element.59), channel_id=1, source_target_pairs={{0,24},{4,28},{8,0},{12,4},{16,8},{20,12},{24,16},{28,20},{1,25},{... | collective-permute-start | bytes 2359304 | tf_op jit(solution)/shard_map/ppermute | solution.py:317
  55.1 27.3 %collective-permute-start.5 = (bf16[400,1024]{1,0:T(8,128)(2,1)S(1)}, bf16[400,1024]{1,0:T(8,128)(2,1)S(1)}, u32[]{:S(2)}, u32[]{:S(2)}) collective-permute-start(bf16[400,1024]{1,0:T(8,128)(2,1)S(1)} %get-tuple-element.49), channel_id=1, source_target_pairs={{0,4},{4,8},{8,12},{12,16},{16,20},{20,24},{24,28},{28,0},{1,5},{5... | collective-permute-start | bytes 2457608 | tf_op jit(solution)/shard_map/ppermute | solution.py:314

commit v4 on v3

--- a/solution.py
+++ b/solution.py
@@ -21,21 +21,27 @@
 
 
 def pack_kernel(*refs):
-    blocks, ids, packed = refs[:2], refs[2:4], refs[4:6]
-    tags, (block_done, tags_done) = refs[6:8], refs[8:]
+    scalars, blocks, ids = refs[:4], refs[4:7], refs[7:10]
+    outs, own = refs[10:13], refs[13:17]
+    tags, at_hand, (block_done, tags_done, scalars_done) = refs[17:20], refs[20:24], refs[24:27]
+    products, weights = refs[27:]
     rows, width = blocks[0].shape
+    odd = lax.axis_index("row") % 2 == 1
     copies = [
         pltpu.make_async_copy(block, out.at[:rows, :], block_done.at[k])
-        for k, (block, out) in enumerate(zip(blocks, packed))
+        for k, (block, out) in enumerate(zip(blocks, outs))
     ]
-    tag_copies = [
+    small = [
         pltpu.make_async_copy(source, tags[k], tags_done.at[k]) for k, source in enumerate(ids)
+    ] + [
+        pltpu.make_async_copy(source, at_hand[k], scalars_done.at[k])
+        for k, source in enumerate(scalars)
     ]
-    for copy in tag_copies + copies:
+    for copy in small + copies:
         copy.start()
-    for copy in tag_copies:
+    for copy in small:
         copy.wait()
-    for k, out in enumerate(packed):
+    for k, out in enumerate(outs[:2]):
         tag = tags[k][...].reshape(1, rows)
         high = tag // TAG_BASE
         low = tag - high * TAG_BASE
@@ -45,22 +51,32 @@
     for copy in copies:
         copy.wait()
 
-
-def pack(blocks, ids):
+    @pl.when(odd)
+    def _():
+        own_meetings(at_hand, outs[0], outs[1], (outs[2], tags[2]), own, products, weights)
+
+
+def pack(scalars, blocks, ids):
     rows, width = blocks[0].shape
     hbm, vmem = pl.BlockSpec(memory_space=pltpu.HBM), pl.BlockSpec(memory_space=pltpu.VMEM)
+    packed, square = pltpu.VMEM((rows + TAG_ROWS, width), BF16), pltpu.VMEM((rows, width), F32)
     return pl.pallas_call(
         pack_kernel,
-        out_shape=[pltpu.VMEM((rows + TAG_ROWS, width), BF16)] * 2,
-        in_specs=[hbm] * 4,
-        out_specs=[vmem] * 2,
+        out_shape=[packed] * 2 + [pltpu.VMEM((rows, width), BF16), pltpu.VMEM((1, rows), F32)]
+        + [square] * 3,
+        in_specs=[hbm] * 10,
+        out_specs=[vmem] * 7,
         scratch_shapes=[
-            *[pltpu.VMEM((rows,), jnp.int32)] * 2,
-            pltpu.SemaphoreType.DMA((2,)),
-            pltpu.SemaphoreType.DMA((2,)),
+            *[pltpu.VMEM((rows,), jnp.int32)] * 3,
+            *[pltpu.SMEM((1,), F32)] * 4,
+            pltpu.SemaphoreType.DMA((3,)),
+            pltpu.SemaphoreType.DMA((3,)),
+            pltpu.SemaphoreType.DMA((4,)),
+            pltpu.VMEM((rows, rows), F32),
+            pltpu.VMEM((rows, rows), BF16),
         ],
-        compiler_params=pltpu.CompilerParams(vmem_limit_bytes=56 * 2**20),
-    )(*blocks, *ids)
+        compiler_params=pltpu.CompilerParams(vmem_limit_bytes=52 * 2**20),
+    )(*scalars, *blocks, *ids)
 
 
 def tags_of(block):
@@ -117,21 +133,33 @@
     return jnp.dot(weights[...], video[: weights.shape[0], part], preferred_element_type=F32)
 
 
-def own_kernel(
-    imu_log_scale, imu_bias, audio_log_scale, audio_bias, video, imu, audio, audio_ids,
-    loss, video_grad, imu_grad, audio_grad, video_on, imu_on, products, weights,
-):
-    video_on[...] = video[...]
-    imu_on[...] = imu[...]
-    audio = (audio, audio_ids)
-    loss[...] = meet(video, audio, (audio_log_scale, audio_bias), products, weights)
+def own_meetings(scalars, video, imu, audio, outs, products, weights):
+    loss, video_grad, imu_grad, audio_grad = outs
+    loss[...] = meet(video, audio, scalars[2:], products, weights)
     for part in column_parts(video):
         video_grad[:, part] = to_video(weights, audio, part)
         audio_grad[:, part] = to_partner(weights, video, part)
-    loss[...] += meet(video, imu, (imu_log_scale, imu_bias), products, weights)
+    loss[...] += meet(video, imu, scalars[:2], products, weights)
     for part in column_parts(video):
         video_grad[:, part] += to_video(weights, imu, part)
         imu_grad[:, part] = to_partner(weights, video, part)
+
+
+def own_kernel(*refs):
+    scalars, (video, imu, audio, audio_ids), made = refs[:4], refs[4:8], refs[8:12]
+    outs, (video_on, imu_on, products, weights) = refs[12:16], refs[16:]
+    even = lax.axis_index("row") % 2 == 0
+    video_on[...] = video[...]
+    imu_on[...] = imu[...]
+
+    @pl.when(even)
+    def _():
+        own_meetings(scalars, video, imu, (audio, audio_ids), outs, products, weights)
+
+    @pl.when(jnp.logical_not(even))
+    def _():
+        for out, value in zip(outs, made):
+            out[...] = value[...]
 
 
 def put_losses(losses, packed):
@@ -327,16 +355,18 @@
     of_imu, of_audio = (imu_log_scale, imu_bias), (audio_log_scale, audio_bias)
     along_row, along_col = Tile("row"), Tile("col")
 
+    video, imu, audio, *made = pack(
+        of_imu + of_audio, (video, imu, audio), (video_ids, imu_ids, audio_ids)
+    )
     col_audio = along_col.bring_partner(audio), along_col.bring_partner(audio_ids)
     audio = (audio, audio_ids)
-    video, imu = pack((video, imu), (video_ids, imu_ids))
     col_video = along_col.bring_video(video)
 
     loss, video_grad, imu_grad, audio_grad, video_on, imu_on = call(
         own_kernel,
         [line, square, square, square, packed, packed],
         of_imu + of_audio,
-        (video, imu, *audio),
+        (video, imu, *audio, *made),
         rows, 1, COSTS["own"],
     )
     row_video = along_row.bring_video(video_on)

time: 83.8 us -> 88.8 us (1.060)
  starting transfers between devices: 13.4 us -> 16.2 us
  waiting for transfers between devices: 47.3 us -> 49 us
    ppermute x3, waiting for transfers between devices: 23.3 us -> 26.3 us  [bring_partner(): return lax.ppermute(block, self.axis, self.partner)]
    ppermute x2, starting transfers between devices: 1.03 us -> 3.42 us  [return_video(): return lax.ppermute(block, self.axis, [(b, a) for a, b in self.video])]
    ppermute x2, waiting for transfers between devices: 22.7 us -> 20.9 us  [return_partner(): return lax.ppermute(block, self.axis, [(b, a) for a, b in self.partner])]
    ppermute x2, waiting for transfers between devices: 0.18 us -> 1.66 us  [return_video(): return lax.ppermute(block, self.axis, [(b, a) for a, b in self.video])]
    ppermute x2, waiting for transfers between devices: 1.16 us -> 0.01 us  [bring_video(): return lax.ppermute(block, self.axis, self.video)]
  transfers between devices with their start and end apart: 9 -> 9, of which waited for: 4 -> 3; matrix products, arithmetic and copies ran while one was open for 0% -> 0% of each run, Pallas kernels for 22% -> 19%
where the time goes in v4:
time: 88.8 us; the launch traced here: 88.6 us
  waiting for transfers between devices  49 us (55%)
  Pallas kernels  19.9 us (22%)
  starting transfers between devices  16.2 us (18%)
  between operations  3.49 us (4%)
    ppermute x3, waiting for transfers between devices, bring_partner(): return lax.ppermute(block, self.axis, self.partner)  26.3 us
    ppermute x2, waiting for transfers between devices, return_partner(): return lax.ppermute(block, self.axis, [(b, a) for a, b in self.partner])  20.9 us
    pallas_call x6, Pallas kernels, call(): pl.pallas_call(kernel, out_shape=[jax.ShapeDtypeStruct(*out) for out in o...  14.3 us
    ppermute x2, starting transfers between devices, return_partner(): return lax.ppermute(block, self.axis, [(b, a) for a, b in self.partner])  5.01 us
    ppermute x3, starting transfers between devices, bring_partner(): return lax.ppermute(block, self.axis, self.partner)  4.55 us
    pallas_call x4, Pallas kernels, summed(): pl.pallas_call(kernel, out_shape=[jax.ShapeDtypeStruct(*out) for out in o...  3.8 us
    ppermute x2, starting transfers between devices, return_video(): return lax.ppermute(block, self.axis, [(b, a) for a, b in self.video])  3.42 us
    ppermute x2, starting transfers between devices, bring_video(): return lax.ppermute(block, self.axis, self.video)  3.25 us
  transfers between devices with their start and end apart: 9, of which 3 were waited for; matrix products, arithmetic and copies ran while one was open for 0% of the time, Pallas kernels for 19%

profile of v4, /device:TPU:0, one launch (start us, length us, event | category | flops | bytes accessed | tf_op | source)
XLA Modules:
  0.0 88.6 jit_solution(5827469324673136454)
XLA Ops:
  0.6 0.0 copy-start
  3.2 1.7 %shard_map.129 = (bf16[400,1024]{1,0:T(8,128)(2,1)S(1)}, bf16[400,1024]{1,0:T(8,128)(2,1)S(1)}, bf16[384,1024]{1,0:T(8,128)(2,1)S(1)}, f32[1,384]{1,0:T(1,128)S(...) custom-call(f32[1]{0:T(128)S(6)} %copy.14.refs_0_.log_scale, ...), custom_call_target="tpu_custom_call" | custom-call | tf_op jit(solution)/shard_map/pallas_call | solution.py:63
  5.0 4.1 %collective-permute-start.3 = (bf16[384,1024]{1,0:T(8,128)(2,1)S(1)}, bf16[384,1024]{1,0:T(8,128)(2,1)S(1)}, u32[]{:S(2)}, u32[]{:S(2)}) collective-permute-start(bf16[384,1024]{1,0:T(8,128)(2,1)S(1)} %get-tuple-element.45.refs_6_.audio), channel_id=1, source_target_pairs={{2,0},{3,1},{0,2},{1,3},{6,4},{7,5},{4,6},{5,7},{10,8},{11,9},{8,1... | collective-permute-start | bytes 2359304 | tf_op jit(solution)/shard_map/ppermute | solution.py:339
  9.1 1.6 %collective-permute-start.2 = (bf16[400,1024]{1,0:T(8,128)(2,1)S(1)}, bf16[400,1024]{1,0:T(8,128)(2,1)S(1)}, u32[]{:S(2)}, u32[]{:S(2)}) collective-permute-start(bf16[400,1024]{1,0:T(8,128)(2,1)S(1)} %get-tuple-element.43.refs_4_.video), channel_id=1, source_target_pairs={{1,0},{0,1},{3,2},{2,3},{5,4},{4,5},{7,6},{6,7},{9,8},{8,9},{11,10... | collective-permute-start | bytes 2457608 | tf_op jit(solution)/shard_map/ppermute | solution.py:336
  10.7 0.0 copy-done
  10.7 3.8 %shard_map.130 = (f32[1,384]{1,0:T(1,128)S(1)}, f32[384,1024]{1,0:T(8,128)S(1)}, f32[384,1024]{1,0:T(8,128)S(1)}, f32[384,1024]{1,0:T(8,128)S(1)}, bf16[400,1024...) custom-call(f32[1]{0:T(128)S(6)} %copy.14.refs_0_.log_scale, f32[1]{0:T(128)S(6)} %copy.15.refs_1_.bias, ...), custom_call_target="tpu_custom_call" | custom-call | flops 500000000 | bytes 14292992 | tf_op jit(solution)/shard_map/pallas_call | solution.py:309
  14.5 1.7 %collective-permute-start = (bf16[400,1024]{1,0:T(8,128)(2,1)S(1)}, bf16[400,1024]{1,0:T(8,128)(2,1)S(1)}, u32[]{:S(2)}, u32[]{:S(2)}) collective-permute-start(bf16[400,1024]{1,0:T(8,128)(2,1)S(1)} %get-tuple-element.50), channel_id=1, source_target_pairs={{4,0},{8,4},{12,8},{16,12},{20,16},{24,20},{28,24},{0,28},{5,1},{9... | collective-permute-start | bytes 2457608 | tf_op jit(solution)/shard_map/ppermute | solution.py:336
  16.2 0.1 collective-permute-start.1
  16.3 0.3 collective-permute-start.4
  16.6 26.3 %collective-permute-done.4.audio_ids = s32[384]{0:T(512)S(1)} collective-permute-done((s32[384]{0:T(512)S(1)}, s32[384]{0:T(512)S(1)}, u32[]{:S(2)}, u32[]{:S(2)}) %collective-permute-start.4) | collective-permute-done | bytes 1568 | tf_op jit(solution)/shard_map/ppermute | solution.py:339
  43.0 0.0 collective-permute-done.3.audio.far_audio
  43.0 1.0 %shard_map.131 = (f32[1,384]{1,0:T(1,128)S(1)}, bf16[384,384]{1,0:T(8,128)(2,1)S(1)}) custom-call(f32[1]{0:T(128)S(6)} %copy.16.refs_2_.log_scale, f32[1]{0:T(128)S(6)} %copy.17.refs_3_.bias, bf16[400,1024]{1,0:T(8,128)(2,1)S(1)} %get-tuple-element.43.refs_4_.video, bf16[384,1024]{1,0:T(8,128)(2,1)S(1)} %collective-permute-done.3.audio.far_audio, ...), custom_call_target="tpu_custom_call" | custom-call | flops 500000000 | bytes 3217408 | tf_op jit(solution)/shard_map/pallas_call | solution.py:309
  44.0 0.0 collective-permute-done.2.other_video.col_video
  44.0 1.9 %shard_map.132 = (f32[1,384]{1,0:T(1,128)S(1)}, f32[1,384]{1,0:T(1,128)S(1)}, bf16[384,1024]{1,0:T(8,128)(2,1)S(1)}, bf16[384,384]{1,0:T(8,128)(2,1)S(1)}) custom-call(f32[1]{0:T(128)S(6)} %copy.16.refs_2_.log_scale, f32[1]{0:T(128)S(6)} %copy.17.refs_3_.bias, bf16[400,1024]{1,0:T(8,128)(2,1)S(1)} %get-tuple-element.43.refs_4_.video, ...), custom_call_target="tpu_custom_call" | custom-call | flops 500000000 | bytes 5445632 | tf_op jit(solution)/shard_map/pallas_call | solution.py:309
  45.9 2.5 %collective-permute-start.8 = (bf16[384,1024]{1,0:T(8,128)(2,1)S(1)}, bf16[384,1024]{1,0:T(8,128)(2,1)S(1)}, u32[]{:S(2)}, u32[]{:S(2)}) collective-permute-start(bf16[384,1024]{1,0:T(8,128)(2,1)S(1)} %get-tuple-element.71), channel_id=1, source_target_pairs={{0,2},{1,3},{2,0},{3,1},{4,6},{5,7},{6,4},{7,5},{8,10},{9,11},{10,... | collective-permute-start | bytes 2359304 | tf_op jit(solution)/shard_map/ppermute | solution.py:345
  48.4 1.8 %shard_map.133 = (bf16[400,1024]{1,0:T(8,128)(2,1)S(1)}, bf16[384,384]{1,0:T(8,128)(2,1)S(1)}, f32[1,384]{1,0:T(1,128)S(1)}) custom-call(f32[1]{0:T(128)S(6)} %copy.16.refs_2_.log_scale, f32[1]{0:T(128)S(6)} %copy.17.refs_3_.bias, bf16[400,1024]{1,0:T(8,128)(2,1)S(1)} %collective-permute-done.2.other_video.col_video, ...), custom_call_target="tpu_custom_call" | custom-call | flops 500000000 | bytes 5383168 | tf_op jit(solution)/shard_map/pallas_call | solution.py:309
  50.2 3.4 %collective-permute-start.6 = (bf16[400,1024]{1,0:T(8,128)(2,1)S(1)}, bf16[400,1024]{1,0:T(8,128)(2,1)S(1)}, u32[]{:S(2)}, u32[]{:S(2)}) collective-permute-start(bf16[400,1024]{1,0:T(8,128)(2,1)S(1)} %get-tuple-element.60), channel_id=1, source_target_pairs={{0,1},{1,0},{2,3},{3,2},{4,5},{5,4},{6,7},{7,6},{8,9},{9,8},{10,11... | collective-permute-start | bytes 2457608 | tf_op jit(solution)/shard_map/ppermute | solution.py:342
  53.6 0.0 collective-permute-done.other_video.row_video
  53.6 0.0 collective-permute-done.1.other_imu.row_imu
  53.6 4.0 %shard_map.134 = (f32[1,384]{1,0:T(1,128)S(1)}, bf16[400,1024]{1,0:T(8,128)(2,1)S(1)}, bf16[384,1024]{1,0:T(8,128)(2,1)S(1)}, bf16[384,384]{1,0:T(8,128)(2,1)S(1)}, bf16[384,384]{1,0:T(8,128)(2,1)S(1)}) custom-call(f32[1]{0:T(128)S(6)} %copy.14.refs_0_.log_scale, f32[1]{0:T(128)S(6)} %copy.15.refs_1_.bias, ...), custom_call_target="tpu_custom_call" | custom-call | flops 500000000 | bytes 6556672 | tf_op jit(solution)/shard_map/pallas_call | solution.py:309
  57.6 2.5 %collective-permute-start.7 = (bf16[384,1024]{1,0:T(8,128)(2,1)S(1)}, bf16[384,1024]{1,0:T(8,128)(2,1)S(1)}, u32[]{:S(2)}, u32[]{:S(2)}) collective-permute-start(bf16[384,1024]{1,0:T(8,128)(2,1)S(1)} %get-tuple-element.69), channel_id=1, source_target_pairs={{0,24},{4,28},{8,0},{12,4},{16,8},{20,12},{24,16},{28,20},{1,25},{... | collective-permute-start | bytes 2359304 | tf_op jit(solution)/shard_map/ppermute | solution.py:345
  60.1 0.0 collective-permute-start.5
  60.1 1.9 %shard_map.135 = (f32[384,1024]{1,0:T(8,128)S(1)}, f32[384,1024]{1,0:T(8,128)S(1)}, f32[384,1024]{1,0:T(8,128)S(1)}, f32[1,384]{1,0:T(1,128)S(1)}) custom-call(bf16[384,1024]{1,0:T(8,128)(2,1)S(1)} %collective-permute-done.3.audio.far_audio, bf16[384,384]{1,0:T(8,128)(2,1)S(1)} %get-tuple-element.53.own_weights.far_weights, ...), custom_call_target="tpu_custom_call" | custom-call | flops 10000000 | bytes 18287616 | tf_op jit(solution)/shard_map/pallas_call | solution.py:309
  62.0 20.9 %collective-permute-done.8.got = bf16[384,1024]{1,0:T(8,128)(2,1)S(1)} collective-permute-done((bf16[384,1024]{1,0:T(8,128)(2,1)S(1)}, bf16[384,1024]{1,0:T(8,128)(2,1)S(1)}, u32[]{:S(2)}, u32[]{:S(2)}) %collective-permute-start.8) | collective-permute-done | bytes 786464 | tf_op jit(solution)/shard_map/ppermute | solution.py:345
  82.9 1.2 %shard_map.136 = (f32[384,1024]{1,0:T(8,128)}, f32[1,384]{1,0:T(1,128)S(1)}) custom-call(bf16[384,1024]{1,0:T(8,128)(2,1)S(1)} %collective-permute-done.8.got, f32[384,1024]{1,0:T(8,128)S(1)} %get-tuple-element.72.grad_in, f32[1,384]{1,0:T(1,128)S(1)} %get-tuple-element.73.loss_in), custom_call_target="tpu_custom_call" | custom-call | flops 5000000000 | tf_op jit(solution)/shard_map/pallas_call | solution.py:286
  84.1 0.0 collective-permute-done.7.got
  84.2 1.2 %shard_map.137 = (f32[384,1024]{1,0:T(8,128)}, f32[1,384]{1,0:T(1,128)S(1)}) custom-call(bf16[384,1024]{1,0:T(8,128)(2,1)S(1)} %collective-permute-done.7.got, f32[384,1024]{1,0:T(8,128)S(1)} %get-tuple-element.70.grad_in, f32[1,384]{1,0:T(1,128)S(1)} %get-tuple-element.74.loss_in), custom_call_target="tpu_custom_call" | custom-call | flops 10000000 | tf_op jit(solution)/shard_map/pallas_call | solution.py:286
  85.4 1.7 %collective-permute-done.6.got_video = bf16[400,1024]{1,0:T(8,128)(2,1)S(1)} collective-permute-done((bf16[400,1024]{1,0:T(8,128)(2,1)S(1)}, bf16[400,1024]{1,0:T(8,128)(2,1)S(1)}, u32[]{:S(2)}, u32[]{:S(2)}) %collective-permute-start.6) | collective-permute-done | bytes 819232 | tf_op jit(solution)/shard_map/ppermute | solution.py:342
  87.0 0.1 shard_map.138
  87.2 0.0 collective-permute-done.5.got_video
  87.2 1.2 %shard_map.139 = (f32[384,1024]{1,0:T(8,128)}, f32[384]{0:T(512)}) custom-call(bf16[400,1024]{1,0:T(8,128)(2,1)S(1)} %collective-permute-done.5.got_video, f32[384,1024]{1,0:T(8,128)S(1)} %get-tuple-element.76.video_in, f32[1,384]{1,0:T(1,128)S(1)} %get-tuple-element.77.loss_in), custom_call_target="tpu_custom_call" | custom-call | flops 500000000 | tf_op jit(solution)/shard_map/pallas_call | solution.py:286
Async XLA Ops:
  0.6 10.0 %copy-start = (s32[384]{0:T(512)S(1)}, s32[384]{0:T(512)}, u32[]{:S(2)}) copy-start(s32[384]{0:T(512)} %audio_ids.1) | copy-start | bytes 4612
  5.0 38.0 %collective-permute-start.3 = (bf16[384,1024]{1,0:T(8,128)(2,1)S(1)}, bf16[384,1024]{1,0:T(8,128)(2,1)S(1)}, u32[]{:S(2)}, u32[]{:S(2)}) collective-permute-start(bf16[384,1024]{1,0:T(8,128)(2,1)S(1)} %get-tuple-element.45.refs_6_.audio), channel_id=1, source_target_pairs={{2,0},{3,1},{0,2},{1,3},{6,4},{7,5},{4,6},{5,7},{10,8},{11,9},{8,1... | collective-permute-start | bytes 2359304 | tf_op jit(solution)/shard_map/ppermute | solution.py:339
  9.1 34.9 %collective-permute-start.2 = (bf16[400,1024]{1,0:T(8,128)(2,1)S(1)}, bf16[400,1024]{1,0:T(8,128)(2,1)S(1)}, u32[]{:S(2)}, u32[]{:S(2)}) collective-permute-start(bf16[400,1024]{1,0:T(8,128)(2,1)S(1)} %get-tuple-element.43.refs_4_.video), channel_id=1, source_target_pairs={{1,0},{0,1},{3,2},{2,3},{5,4},{4,5},{7,6},{6,7},{9,8},{8,9},{11,10... | collective-permute-start | bytes 2457608 | tf_op jit(solution)/shard_map/ppermute | solution.py:336
  14.5 39.1 %collective-permute-start = (bf16[400,1024]{1,0:T(8,128)(2,1)S(1)}, bf16[400,1024]{1,0:T(8,128)(2,1)S(1)}, u32[]{:S(2)}, u32[]{:S(2)}) collective-permute-start(bf16[400,1024]{1,0:T(8,128)(2,1)S(1)} %get-tuple-element.50), channel_id=1, source_target_pairs={{4,0},{8,4},{12,8},{16,12},{20,16},{24,20},{28,24},{0,28},{5,1},{9... | collective-permute-start | bytes 2457608 | tf_op jit(solution)/shard_map/ppermute | solution.py:336
  16.2 37.4 %collective-permute-start.1 = (bf16[400,1024]{1,0:T(8,128)(2,1)S(1)}, bf16[400,1024]{1,0:T(8,128)(2,1)S(1)}, u32[]{:S(2)}, u32[]{:S(2)}) collective-permute-start(bf16[400,1024]{1,0:T(8,128)(2,1)S(1)} %get-tuple-element.51), channel_id=1, source_target_pairs={{24,0},{28,4},{0,8},{4,12},{8,16},{12,20},{16,24},{20,28},{25,1},{... | collective-permute-start | bytes 2457608 | tf_op jit(solution)/shard_map/ppermute | solution.py:339
  16.3 26.7 %collective-permute-start.4 = (s32[384]{0:T(512)S(1)}, s32[384]{0:T(512)S(1)}, u32[]{:S(2)}, u32[]{:S(2)}) collective-permute-start(s32[384]{0:T(512)S(1)} %copy-done), channel_id=1, source_target_pairs={{2,0},{3,1},{0,2},{1,3},{6,4},{7,5},{4,6},{5,7},{10,8},{11,9},{8,1... | collective-permute-start | bytes 4616 | tf_op jit(solution)/shard_map/ppermute | solution.py:339
  45.9 37.0 %collective-permute-start.8 = (bf16[384,1024]{1,0:T(8,128)(2,1)S(1)}, bf16[384,1024]{1,0:T(8,128)(2,1)S(1)}, u32[]{:S(2)}, u32[]{:S(2)}) collective-permute-start(bf16[384,1024]{1,0:T(8,128)(2,1)S(1)} %get-tuple-element.71), channel_id=1, source_target_pairs={{0,2},{1,3},{2,0},{3,1},{4,6},{5,7},{6,4},{7,5},{8,10},{9,11},{10,... | collective-permute-start | bytes 2359304 | tf_op jit(solution)/shard_map/ppermute | solution.py:345
  50.2 36.8 %collective-permute-start.6 = (bf16[400,1024]{1,0:T(8,128)(2,1)S(1)}, bf16[400,1024]{1,0:T(8,128)(2,1)S(1)}, u32[]{:S(2)}, u32[]{:S(2)}) collective-permute-start(bf16[400,1024]{1,0:T(8,128)(2,1)S(1)} %get-tuple-element.60), channel_id=1, source_target_pairs={{0,1},{1,0},{2,3},{3,2},{4,5},{5,4},{6,7},{7,6},{8,9},{9,8},{10,11... | collective-permute-start | bytes 2457608 | tf_op jit(solution)/shard_map/ppermute | solution.py:342
  57.6 26.5 %collective-permute-start.7 = (bf16[384,1024]{1,0:T(8,128)(2,1)S(1)}, bf16[384,1024]{1,0:T(8,128)(2,1)S(1)}, u32[]{:S(2)}, u32[]{:S(2)}) collective-permute-start(bf16[384,1024]{1,0:T(8,128)(2,1)S(1)} %get-tuple-element.69), channel_id=1, source_target_pairs={{0,24},{4,28},{8,0},{12,4},{16,8},{20,12},{24,16},{28,20},{1,25},{... | collective-permute-start | bytes 2359304 | tf_op jit(solution)/shard_map/ppermute | solution.py:345
  60.1 27.1 %collective-permute-start.5 = (bf16[400,1024]{1,0:T(8,128)(2,1)S(1)}, bf16[400,1024]{1,0:T(8,128)(2,1)S(1)}, u32[]{:S(2)}, u32[]{:S(2)}) collective-permute-start(bf16[400,1024]{1,0:T(8,128)(2,1)S(1)} %get-tuple-element.59), channel_id=1, source_target_pairs={{0,4},{4,8},{8,12},{12,16},{16,20},{20,24},{24,28},{28,0},{1,5},{5... | collective-permute-start | bytes 2457608 | tf_op jit(solution)/shard_map/ppermute | solution.py:342

commit v5 on v3

--- a/solution.py
+++ b/solution.py
@@ -7,7 +7,7 @@
 
 STEPS = 4
 SLAB = 16
-COLUMNS = 512
+COLUMNS = 1024
 SUM_BLOCKS = 4
 TAG_ROWS = 16
 TAG_BASE = 256

time: 83.8 us -> 83.7 us (level)
  no operation moved by 1% of the time
where the time goes in v5:
time: 83.7 us; the launch traced here: 83.5 us
  waiting for transfers between devices  47.4 us (57%)
  Pallas kernels  19.3 us (23%)
  starting transfers between devices  13.4 us (16%)
  between operations  3.34 us (4%)
    ppermute x3, waiting for transfers between devices, bring_partner(): return lax.ppermute(block, self.axis, self.partner)  23.2 us
    ppermute x2, waiting for transfers between devices, return_partner(): return lax.ppermute(block, self.axis, [(b, a) for a, b in self.partner])  22.9 us
    pallas_call x6, Pallas kernels, call(): pl.pallas_call(kernel, out_shape=[jax.ShapeDtypeStruct(*out) for out in o...  14.1 us
    ppermute x2, starting transfers between devices, return_partner(): return lax.ppermute(block, self.axis, [(b, a) for a, b in self.partner])  4.69 us
    ppermute x3, starting transfers between devices, bring_partner(): return lax.ppermute(block, self.axis, self.partner)  4.67 us
    pallas_call x4, Pallas kernels, summed(): pl.pallas_call(kernel, out_shape=[jax.ShapeDtypeStruct(*out) for out in o...  3.8 us
    ppermute x2, starting transfers between devices, bring_video(): return lax.ppermute(block, self.axis, self.video)  3.02 us
  transfers between devices with their start and end apart: 9, of which 4 were waited for; matrix products, arithmetic and copies ran while one was open for 0% of the time, Pallas kernels for 22%

profile of v5, /device:TPU:0, one launch (start us, length us, event | category | flops | bytes accessed | tf_op | source)
XLA Modules:
  0.0 83.5 jit_solution(4842229847913979864)
XLA Ops:
  0.6 0.0 copy-start
  0.6 0.0 copy-start.1
  0.7 4.1 %collective-permute-start.3 = (bf16[384,1024]{1,0:T(8,128)(2,1)}, bf16[384,1024]{1,0:T(8,128)(2,1)S(1)}, u32[]{:S(2)}, u32[]{:S(2)}) collective-permute-start(bf16[384,1024]{1,0:T(8,128)(2,1)} %audio.3), channel_id=1, source_target_pairs={{2,0},{3,1},{0,2},{1,3},{6,4},{7,5},{4,6},{5,7},{10,8},{11,9},{8,1... | collective-permute-start | bytes 2359304 | tf_op jit(solution)/shard_map/ppermute | solution.py:311
  4.8 1.4 %shard_map.129 = (bf16[400,1024]{1,0:T(8,128)(2,1)S(1)}, bf16[400,1024]{1,0:T(8,128)(2,1)S(1)}) custom-call(bf16[384,1024]{1,0:T(8,128)(2,1)} %refs_0_.1, bf16[384,1024]{1,0:T(8,128)(2,1)} %refs_1_.1, s32[384]{0:T(512)} %refs_2_.1, s32[384]{0:T(512)} %refs_3_.1), custom_call_target="tpu_custom_call" | custom-call | tf_op jit(solution)/shard_map/pallas_call | solution.py:52
  6.2 1.6 %collective-permute-start.2 = (bf16[400,1024]{1,0:T(8,128)(2,1)S(1)}, bf16[400,1024]{1,0:T(8,128)(2,1)S(1)}, u32[]{:S(2)}, u32[]{:S(2)}) collective-permute-start(bf16[400,1024]{1,0:T(8,128)(2,1)S(1)} %get-tuple-element.38.video), channel_id=1, source_target_pairs={{1,0},{0,1},{3,2},{2,3},{5,4},{4,5},{7,6},{6,7},{9,8},{8,9},{11,10... | collective-permute-start | bytes 2457608 | tf_op jit(solution)/shard_map/ppermute | solution.py:308
  10.4 0.0 copy-done
  10.4 0.0 copy-done.1
  10.5 3.9 %shard_map.130 = (f32[1,384]{1,0:T(1,128)S(1)}, f32[384,1024]{1,0:T(8,128)S(1)}, f32[384,1024]{1,0:T(8,128)S(1)}, f32[384,1024]{1,0:T(8,128)S(1)}, bf16[400,1024...) custom-call(f32[1]{0:T(128)S(6)} %copy.14.imu_log_scale.log_scale, f32[1]{0:T(128)S(6)} %copy.15.imu_bias.bias, ...), custom_call_target="tpu_custom_call" | custom-call | flops 500000000 | bytes 4852736 | tf_op jit(solution)/shard_map/pallas_call | solution.py:281
  14.3 1.4 %collective-permute-start = (bf16[400,1024]{1,0:T(8,128)(2,1)S(1)}, bf16[400,1024]{1,0:T(8,128)(2,1)S(1)}, u32[]{:S(2)}, u32[]{:S(2)}) collective-permute-start(bf16[400,1024]{1,0:T(8,128)(2,1)S(1)} %get-tuple-element.40), channel_id=1, source_target_pairs={{4,0},{8,4},{12,8},{16,12},{20,16},{24,20},{28,24},{0,28},{5,1},{9... | collective-permute-start | bytes 2457608 | tf_op jit(solution)/shard_map/ppermute | solution.py:308
  15.7 0.2 collective-permute-start.1
  15.9 0.3 collective-permute-start.4
  16.3 23.2 %collective-permute-done.4.audio_ids = s32[384]{0:T(512)S(1)} collective-permute-done((s32[384]{0:T(512)S(1)}, s32[384]{0:T(512)S(1)}, u32[]{:S(2)}, u32[]{:S(2)}) %collective-permute-start.4) | collective-permute-done | bytes 1568 | tf_op jit(solution)/shard_map/ppermute | solution.py:311
  39.5 0.0 collective-permute-done.3.audio.far_audio
  39.5 1.0 %shard_map.131 = (f32[1,384]{1,0:T(1,128)S(1)}, bf16[384,384]{1,0:T(8,128)(2,1)S(1)}) custom-call(f32[1]{0:T(128)S(6)} %copy.16.audio_log_scale.log_scale, f32[1]{0:T(128)S(6)} %copy.17.audio_bias.bias, bf16[400,1024]{1,0:T(8,128)(2,1)S(1)} %get-tuple-element.38.video, bf16[384,1024]{1,0:T(8,128)(2,1)S(1)} %collective-permute-done.3.audio.far_audio, ...), custom_call_target="tpu_custom_call" | custom-call | flops 500000000 | bytes 3217408 | tf_op jit(solution)/shard_map/pallas_call | solution.py:281
  40.5 1.2 %collective-permute-done.2.other_video.col_video = bf16[400,1024]{1,0:T(8,128)(2,1)S(1)} collective-permute-done((bf16[400,1024]{1,0:T(8,128)(2,1)S(1)}, bf16[400,1024]{1,0:T(8,128)(2,1)S(1)}, u32[]{:S(2)}, u32[]{:S(2)}) %collective-permute-start.2) | collective-permute-done | bytes 819232 | tf_op jit(solution)/shard_map/ppermute | solution.py:308
  41.7 1.9 %shard_map.132 = (f32[1,384]{1,0:T(1,128)S(1)}, f32[1,384]{1,0:T(1,128)S(1)}, bf16[384,1024]{1,0:T(8,128)(2,1)S(1)}, bf16[384,384]{1,0:T(8,128)(2,1)S(1)}) custom-call(f32[1]{0:T(128)S(6)} %copy.16.audio_log_scale.log_scale, f32[1]{0:T(128)S(6)} %copy.17.audio_bias.bias, bf16[400,1024]{1,0:T(8,128)(2,1)S(1)} %get-tuple-element.38.video, ...), custom_call_target="tpu_custom_call" | custom-call | flops 500000000 | bytes 5445632 | tf_op jit(solution)/shard_map/pallas_call | solution.py:281
  43.6 2.2 %collective-permute-start.8 = (bf16[384,1024]{1,0:T(8,128)(2,1)S(1)}, bf16[384,1024]{1,0:T(8,128)(2,1)S(1)}, u32[]{:S(2)}, u32[]{:S(2)}) collective-permute-start(bf16[384,1024]{1,0:T(8,128)(2,1)S(1)} %get-tuple-element.61), channel_id=1, source_target_pairs={{0,2},{1,3},{2,0},{3,1},{4,6},{5,7},{6,4},{7,5},{8,10},{9,11},{10,... | collective-permute-start | bytes 2359304 | tf_op jit(solution)/shard_map/ppermute | solution.py:317
  45.8 1.7 %shard_map.133 = (bf16[400,1024]{1,0:T(8,128)(2,1)S(1)}, bf16[384,384]{1,0:T(8,128)(2,1)S(1)}, f32[1,384]{1,0:T(1,128)S(1)}) custom-call(f32[1]{0:T(128)S(6)} %copy.16.audio_log_scale.log_scale, f32[1]{0:T(128)S(6)} %copy.17.audio_bias.bias, bf16[400,1024]{1,0:T(8,128)(2,1)S(1)} %collective-permute-done.2.other_video.col_video, ...), custom_call_target="tpu_custom_call" | custom-call | flops 500000000 | bytes 5383168 | tf_op jit(solution)/shard_map/pallas_call | solution.py:281
  47.5 1.0 %collective-permute-start.6 = (bf16[400,1024]{1,0:T(8,128)(2,1)S(1)}, bf16[400,1024]{1,0:T(8,128)(2,1)S(1)}, u32[]{:S(2)}, u32[]{:S(2)}) collective-permute-start(bf16[400,1024]{1,0:T(8,128)(2,1)S(1)} %get-tuple-element.50), channel_id=1, source_target_pairs={{0,1},{1,0},{2,3},{3,2},{4,5},{5,4},{6,7},{7,6},{8,9},{9,8},{10,11... | collective-permute-start | bytes 2457608 | tf_op jit(solution)/shard_map/ppermute | solution.py:314
  48.5 0.0 collective-permute-done.other_video.row_video
  48.5 0.0 collective-permute-done.1.other_imu.row_imu
  48.5 3.8 %shard_map.134 = (f32[1,384]{1,0:T(1,128)S(1)}, bf16[400,1024]{1,0:T(8,128)(2,1)S(1)}, bf16[384,1024]{1,0:T(8,128)(2,1)S(1)}, bf16[384,384]{1,0:T(8,128)(2,1)S(1)}, bf16[384,384]{1,0:T(8,128)(2,1)S(1)}) custom-call(f32[1]{0:T(128)S(6)} %copy.14.imu_log_scale.log_scale, f32[1]{0:T(128)S(6)} %copy.15.imu_bias.bias, ...), custom_call_target="tpu_custom_call" | custom-call | flops 500000000 | bytes 6556672 | tf_op jit(solution)/shard_map/pallas_call | solution.py:281
  52.3 2.5 %collective-permute-start.7 = (bf16[384,1024]{1,0:T(8,128)(2,1)S(1)}, bf16[384,1024]{1,0:T(8,128)(2,1)S(1)}, u32[]{:S(2)}, u32[]{:S(2)}) collective-permute-start(bf16[384,1024]{1,0:T(8,128)(2,1)S(1)} %get-tuple-element.59), channel_id=1, source_target_pairs={{0,24},{4,28},{8,0},{12,4},{16,8},{20,12},{24,16},{28,20},{1,25},{... | collective-permute-start | bytes 2359304 | tf_op jit(solution)/shard_map/ppermute | solution.py:317
  54.8 0.0 collective-permute-start.5
  54.8 1.9 %shard_map.135 = (f32[384,1024]{1,0:T(8,128)S(1)}, f32[384,1024]{1,0:T(8,128)S(1)}, f32[384,1024]{1,0:T(8,128)S(1)}, f32[1,384]{1,0:T(1,128)S(1)}) custom-call(bf16[384,1024]{1,0:T(8,128)(2,1)S(1)} %collective-permute-done.3.audio.far_audio, bf16[384,384]{1,0:T(8,128)(2,1)S(1)} %get-tuple-element.43.own_weights.far_weights, ...), custom_call_target="tpu_custom_call" | custom-call | flops 10000000 | bytes 18287616 | tf_op jit(solution)/shard_map/pallas_call | solution.py:281
  56.7 22.9 %collective-permute-done.8.got = bf16[384,1024]{1,0:T(8,128)(2,1)S(1)} collective-permute-done((bf16[384,1024]{1,0:T(8,128)(2,1)S(1)}, bf16[384,1024]{1,0:T(8,128)(2,1)S(1)}, u32[]{:S(2)}, u32[]{:S(2)}) %collective-permute-start.8) | collective-permute-done | bytes 786464 | tf_op jit(solution)/shard_map/ppermute | solution.py:317
  79.6 1.2 %shard_map.136 = (f32[384,1024]{1,0:T(8,128)}, f32[1,384]{1,0:T(1,128)S(1)}) custom-call(bf16[384,1024]{1,0:T(8,128)(2,1)S(1)} %collective-permute-done.8.got, f32[384,1024]{1,0:T(8,128)S(1)} %get-tuple-element.62.grad_in, f32[1,384]{1,0:T(1,128)S(1)} %get-tuple-element.63.loss_in), custom_call_target="tpu_custom_call" | custom-call | flops 5000000000 | tf_op jit(solution)/shard_map/pallas_call | solution.py:258
  80.8 0.0 collective-permute-done.7.got
  80.8 1.2 %shard_map.137 = (f32[384,1024]{1,0:T(8,128)}, f32[1,384]{1,0:T(1,128)S(1)}) custom-call(bf16[384,1024]{1,0:T(8,128)(2,1)S(1)} %collective-permute-done.7.got, f32[384,1024]{1,0:T(8,128)S(1)} %get-tuple-element.60.grad_in, f32[1,384]{1,0:T(1,128)S(1)} %get-tuple-element.64.loss_in), custom_call_target="tpu_custom_call" | custom-call | flops 10000000 | tf_op jit(solution)/shard_map/pallas_call | solution.py:258
  82.1 0.1 collective-permute-done.6.got_video
  82.1 0.1 shard_map.138
  82.3 0.0 collective-permute-done.5.got_video
  82.3 1.2 %shard_map.139 = (f32[384,1024]{1,0:T(8,128)}, f32[384]{0:T(512)}) custom-call(bf16[400,1024]{1,0:T(8,128)(2,1)S(1)} %collective-permute-done.5.got_video, f32[384,1024]{1,0:T(8,128)S(1)} %get-tuple-element.66.video_in, f32[1,384]{1,0:T(1,128)S(1)} %get-tuple-element.67.loss_in), custom_call_target="tpu_custom_call" | custom-call | flops 500000000 | tf_op jit(solution)/shard_map/pallas_call | solution.py:258
Async XLA Ops:
  0.6 9.8 %copy-start = (bf16[384,1024]{1,0:T(8,128)(2,1)S(1)}, bf16[384,1024]{1,0:T(8,128)(2,1)}, u32[]{:S(2)}) copy-start(bf16[384,1024]{1,0:T(8,128)(2,1)} %audio.3) | copy-start | bytes 2359300
  0.6 9.8 %copy-start.1 = (s32[384]{0:T(512)S(1)}, s32[384]{0:T(512)}, u32[]{:S(2)}) copy-start(s32[384]{0:T(512)} %audio_ids.3) | copy-start | bytes 4612
  0.7 38.9 %collective-permute-start.3 = (bf16[384,1024]{1,0:T(8,128)(2,1)}, bf16[384,1024]{1,0:T(8,128)(2,1)S(1)}, u32[]{:S(2)}, u32[]{:S(2)}) collective-permute-start(bf16[384,1024]{1,0:T(8,128)(2,1)} %audio.3), channel_id=1, source_target_pairs={{2,0},{3,1},{0,2},{1,3},{6,4},{7,5},{4,6},{5,7},{10,8},{11,9},{8,1... | collective-permute-start | bytes 2359304 | tf_op jit(solution)/shard_map/ppermute | solution.py:311
  6.2 35.5 %collective-permute-start.2 = (bf16[400,1024]{1,0:T(8,128)(2,1)S(1)}, bf16[400,1024]{1,0:T(8,128)(2,1)S(1)}, u32[]{:S(2)}, u32[]{:S(2)}) collective-permute-start(bf16[400,1024]{1,0:T(8,128)(2,1)S(1)} %get-tuple-element.38.video), channel_id=1, source_target_pairs={{1,0},{0,1},{3,2},{2,3},{5,4},{4,5},{7,6},{6,7},{9,8},{8,9},{11,10... | collective-permute-start | bytes 2457608 | tf_op jit(solution)/shard_map/ppermute | solution.py:308
  14.3 34.2 %collective-permute-start = (bf16[400,1024]{1,0:T(8,128)(2,1)S(1)}, bf16[400,1024]{1,0:T(8,128)(2,1)S(1)}, u32[]{:S(2)}, u32[]{:S(2)}) collective-permute-start(bf16[400,1024]{1,0:T(8,128)(2,1)S(1)} %get-tuple-element.40), channel_id=1, source_target_pairs={{4,0},{8,4},{12,8},{16,12},{20,16},{24,20},{28,24},{0,28},{5,1},{9... | collective-permute-start | bytes 2457608 | tf_op jit(solution)/shard_map/ppermute | solution.py:308
  15.7 32.8 %collective-permute-start.1 = (bf16[400,1024]{1,0:T(8,128)(2,1)S(1)}, bf16[400,1024]{1,0:T(8,128)(2,1)S(1)}, u32[]{:S(2)}, u32[]{:S(2)}) collective-permute-start(bf16[400,1024]{1,0:T(8,128)(2,1)S(1)} %get-tuple-element.41), channel_id=1, source_target_pairs={{24,0},{28,4},{0,8},{4,12},{8,16},{12,20},{16,24},{20,28},{25,1},{... | collective-permute-start | bytes 2457608 | tf_op jit(solution)/shard_map/ppermute | solution.py:311
  15.9 23.6 %collective-permute-start.4 = (s32[384]{0:T(512)S(1)}, s32[384]{0:T(512)S(1)}, u32[]{:S(2)}, u32[]{:S(2)}) collective-permute-start(s32[384]{0:T(512)S(1)} %copy-done.1), channel_id=1, source_target_pairs={{2,0},{3,1},{0,2},{1,3},{6,4},{7,5},{4,6},{5,7},{10,8},{11,9},{8,1... | collective-permute-start | bytes 4616 | tf_op jit(solution)/shard_map/ppermute | solution.py:311
  43.6 36.0 %collective-permute-start.8 = (bf16[384,1024]{1,0:T(8,128)(2,1)S(1)}, bf16[384,1024]{1,0:T(8,128)(2,1)S(1)}, u32[]{:S(2)}, u32[]{:S(2)}) collective-permute-start(bf16[384,1024]{1,0:T(8,128)(2,1)S(1)} %get-tuple-element.61), channel_id=1, source_target_pairs={{0,2},{1,3},{2,0},{3,1},{4,6},{5,7},{6,4},{7,5},{8,10},{9,11},{10,... | collective-permute-start | bytes 2359304 | tf_op jit(solution)/shard_map/ppermute | solution.py:317
  47.5 34.7 %collective-permute-start.6 = (bf16[400,1024]{1,0:T(8,128)(2,1)S(1)}, bf16[400,1024]{1,0:T(8,128)(2,1)S(1)}, u32[]{:S(2)}, u32[]{:S(2)}) collective-permute-start(bf16[400,1024]{1,0:T(8,128)(2,1)S(1)} %get-tuple-element.50), channel_id=1, source_target_pairs={{0,1},{1,0},{2,3},{3,2},{4,5},{5,4},{6,7},{7,6},{8,9},{9,8},{10,11... | collective-permute-start | bytes 2457608 | tf_op jit(solution)/shard_map/ppermute | solution.py:314
  52.3 28.5 %collective-permute-start.7 = (bf16[384,1024]{1,0:T(8,128)(2,1)S(1)}, bf16[384,1024]{1,0:T(8,128)(2,1)S(1)}, u32[]{:S(2)}, u32[]{:S(2)}) collective-permute-start(bf16[384,1024]{1,0:T(8,128)(2,1)S(1)} %get-tuple-element.59), channel_id=1, source_target_pairs={{0,24},{4,28},{8,0},{12,4},{16,8},{20,12},{24,16},{28,20},{1,25},{... | collective-permute-start | bytes 2359304 | tf_op jit(solution)/shard_map/ppermute | solution.py:317
  54.8 27.5 %collective-permute-start.5 = (bf16[400,1024]{1,0:T(8,128)(2,1)S(1)}, bf16[400,1024]{1,0:T(8,128)(2,1)S(1)}, u32[]{:S(2)}, u32[]{:S(2)}) collective-permute-start(bf16[400,1024]{1,0:T(8,128)(2,1)S(1)} %get-tuple-element.49), channel_id=1, source_target_pairs={{0,4},{4,8},{8,12},{12,16},{16,20},{20,24},{24,28},{28,0},{1,5},{5... | collective-permute-start | bytes 2457608 | tf_op jit(solution)/shard_map/ppermute | solution.py:314

commit v6 on v5

--- a/solution.py
+++ b/solution.py
@@ -299,7 +299,7 @@
         devices = lax.axis_size(axis)
         if devices == STEPS:
             self.video = [(p ^ 1, p) for p in range(devices)]
-            self.partner = [(p ^ 2, p) for p in range(devices)]
+            self.partner = [(p ^ 3, p) for p in range(devices)]
         else:
             self.video = [((p + 1) % devices, p) for p in range(devices)]
             self.partner = [((p - 2) % devices, p) for p in range(devices)]

time: 83.7 us -> 83.7 us (level)
    ppermute x2, waiting for transfers between devices: 22.9 us -> 14.9 us  [return_partner(): return lax.ppermute(block, self.axis, [(b, a) for a, b in self.partner])]
    ppermute x2, waiting for transfers between devices: 0.06 us -> 7.09 us  [return_video(): return lax.ppermute(block, self.axis, [(b, a) for a, b in self.video])]
    ppermute x3, waiting for transfers between devices: 23.2 us -> 25 us  [bring_partner(): return lax.ppermute(block, self.axis, self.partner)]
    ppermute x2, starting transfers between devices: 4.69 us -> 6.05 us  [return_partner(): return lax.ppermute(block, self.axis, [(b, a) for a, b in self.partner])]
    ppermute x2, starting transfers between devices: 3.02 us -> 1.73 us  [bring_video(): return lax.ppermute(block, self.axis, self.video)]
    ppermute x3, starting transfers between devices: 4.67 us -> 5.96 us  [bring_partner(): return lax.ppermute(block, self.axis, self.partner)]
    ppermute x2, waiting for transfers between devices: 1.16 us -> 0.01 us  [bring_video(): return lax.ppermute(block, self.axis, self.video)]
    ppermute x2, starting transfers between devices: 1.03 us -> 0.07 us  [return_video(): return lax.ppermute(block, self.axis, [(b, a) for a, b in self.video])]
where the time goes in v6:
time: 83.7 us; the launch traced here: 83.5 us
  waiting for transfers between devices  47 us (56%)
  Pallas kernels  19.3 us (23%)
  starting transfers between devices  13.8 us (16%)
  between operations  3.37 us (4%)
    ppermute x3, waiting for transfers between devices, bring_partner(): return lax.ppermute(block, self.axis, self.partner)  25 us
    ppermute x2, waiting for transfers between devices, return_partner(): return lax.ppermute(block, self.axis, [(b, a) for a, b in self.partner])  14.9 us
    pallas_call x6, Pallas kernels, call(): pl.pallas_call(kernel, out_shape=[jax.ShapeDtypeStruct(*out) for out in o...  14.1 us
    ppermute x2, waiting for transfers between devices, return_video(): return lax.ppermute(block, self.axis, [(b, a) for a, b in self.video])  7.09 us
    ppermute x2, starting transfers between devices, return_partner(): return lax.ppermute(block, self.axis, [(b, a) for a, b in self.partner])  6.05 us
    ppermute x3, starting transfers between devices, bring_partner(): return lax.ppermute(block, self.axis, self.partner)  5.96 us
    pallas_call x4, Pallas kernels, summed(): pl.pallas_call(kernel, out_shape=[jax.ShapeDtypeStruct(*out) for out in o...  3.79 us
    ppermute x2, starting transfers between devices, bring_video(): return lax.ppermute(block, self.axis, self.video)  1.73 us
  transfers between devices with their start and end apart: 9, of which 4 were waited for; matrix products, arithmetic and copies ran while one was open for 0% of the time, Pallas kernels for 22%

profile of v6, /device:TPU:0, one launch (start us, length us, event | category | flops | bytes accessed | tf_op | source)
XLA Modules:
  0.0 83.5 jit_solution(12197536238221486477)
XLA Ops:
  0.6 0.0 copy-start
  0.6 0.0 copy-start.1
  0.7 5.1 %collective-permute-start.3 = (bf16[384,1024]{1,0:T(8,128)(2,1)}, bf16[384,1024]{1,0:T(8,128)(2,1)S(1)}, u32[]{:S(2)}, u32[]{:S(2)}) collective-permute-start(bf16[384,1024]{1,0:T(8,128)(2,1)} %audio.3), channel_id=1, source_target_pairs={{3,0},{2,1},{1,2},{0,3},{7,4},{6,5},{5,6},{4,7},{11,8},{10,9},{9,1... | collective-permute-start | bytes 2359304 | tf_op jit(solution)/shard_map/ppermute | solution.py:311
  5.8 1.4 %shard_map.129 = (bf16[400,1024]{1,0:T(8,128)(2,1)S(1)}, bf16[400,1024]{1,0:T(8,128)(2,1)S(1)}) custom-call(bf16[384,1024]{1,0:T(8,128)(2,1)} %refs_0_.1, bf16[384,1024]{1,0:T(8,128)(2,1)} %refs_1_.1, s32[384]{0:T(512)} %refs_2_.1, s32[384]{0:T(512)} %refs_3_.1), custom_call_target="tpu_custom_call" | custom-call | tf_op jit(solution)/shard_map/pallas_call | solution.py:52
  7.2 0.1 collective-permute-start.2
  9.9 0.0 copy-done
  9.9 0.0 copy-done.1
  9.9 3.9 %shard_map.130 = (f32[1,384]{1,0:T(1,128)S(1)}, f32[384,1024]{1,0:T(8,128)S(1)}, f32[384,1024]{1,0:T(8,128)S(1)}, f32[384,1024]{1,0:T(8,128)S(1)}, bf16[400,1024...) custom-call(f32[1]{0:T(128)S(6)} %copy.14.imu_log_scale.log_scale, f32[1]{0:T(128)S(6)} %copy.15.imu_bias.bias, ...), custom_call_target="tpu_custom_call" | custom-call | flops 500000000 | bytes 4852736 | tf_op jit(solution)/shard_map/pallas_call | solution.py:281
  13.8 1.7 %collective-permute-start = (bf16[400,1024]{1,0:T(8,128)(2,1)S(1)}, bf16[400,1024]{1,0:T(8,128)(2,1)S(1)}, u32[]{:S(2)}, u32[]{:S(2)}) collective-permute-start(bf16[400,1024]{1,0:T(8,128)(2,1)S(1)} %get-tuple-element.40), channel_id=1, source_target_pairs={{4,0},{8,4},{12,8},{16,12},{20,16},{24,20},{28,24},{0,28},{5,1},{9... | collective-permute-start | bytes 2457608 | tf_op jit(solution)/shard_map/ppermute | solution.py:308
  15.4 0.0 collective-permute-start.1
  15.4 0.8 %collective-permute-start.4 = (s32[384]{0:T(512)S(1)}, s32[384]{0:T(512)S(1)}, u32[]{:S(2)}, u32[]{:S(2)}) collective-permute-start(s32[384]{0:T(512)S(1)} %copy-done.1), channel_id=1, source_target_pairs={{3,0},{2,1},{1,2},{0,3},{7,4},{6,5},{5,6},{4,7},{11,8},{10,9},{9,1... | collective-permute-start | bytes 4616 | tf_op jit(solution)/shard_map/ppermute | solution.py:311
  16.3 24.9 %collective-permute-done.4.audio_ids = s32[384]{0:T(512)S(1)} collective-permute-done((s32[384]{0:T(512)S(1)}, s32[384]{0:T(512)S(1)}, u32[]{:S(2)}, u32[]{:S(2)}) %collective-permute-start.4) | collective-permute-done | bytes 1568 | tf_op jit(solution)/shard_map/ppermute | solution.py:311
  41.2 0.0 collective-permute-done.3.audio.far_audio
  41.2 1.0 %shard_map.131 = (f32[1,384]{1,0:T(1,128)S(1)}, bf16[384,384]{1,0:T(8,128)(2,1)S(1)}) custom-call(f32[1]{0:T(128)S(6)} %copy.16.audio_log_scale.log_scale, f32[1]{0:T(128)S(6)} %copy.17.audio_bias.bias, bf16[400,1024]{1,0:T(8,128)(2,1)S(1)} %get-tuple-element.38.video, bf16[384,1024]{1,0:T(8,128)(2,1)S(1)} %collective-permute-done.3.audio.far_audio, ...), custom_call_target="tpu_custom_call" | custom-call | flops 500000000 | bytes 3217408 | tf_op jit(solution)/shard_map/pallas_call | solution.py:281
  42.2 0.0 collective-permute-done.2.other_video.col_video
  42.3 1.9 %shard_map.132 = (f32[1,384]{1,0:T(1,128)S(1)}, f32[1,384]{1,0:T(1,128)S(1)}, bf16[384,1024]{1,0:T(8,128)(2,1)S(1)}, bf16[384,384]{1,0:T(8,128)(2,1)S(1)}) custom-call(f32[1]{0:T(128)S(6)} %copy.16.audio_log_scale.log_scale, f32[1]{0:T(128)S(6)} %copy.17.audio_bias.bias, bf16[400,1024]{1,0:T(8,128)(2,1)S(1)} %get-tuple-element.38.video, ...), custom_call_target="tpu_custom_call" | custom-call | flops 500000000 | bytes 5445632 | tf_op jit(solution)/shard_map/pallas_call | solution.py:281
  44.2 3.6 %collective-permute-start.8 = (bf16[384,1024]{1,0:T(8,128)(2,1)S(1)}, bf16[384,1024]{1,0:T(8,128)(2,1)S(1)}, u32[]{:S(2)}, u32[]{:S(2)}) collective-permute-start(bf16[384,1024]{1,0:T(8,128)(2,1)S(1)} %get-tuple-element.61), channel_id=1, source_target_pairs={{0,3},{1,2},{2,1},{3,0},{4,7},{5,6},{6,5},{7,4},{8,11},{9,10},{10,... | collective-permute-start | bytes 2359304 | tf_op jit(solution)/shard_map/ppermute | solution.py:317
  47.7 1.7 %shard_map.133 = (bf16[400,1024]{1,0:T(8,128)(2,1)S(1)}, bf16[384,384]{1,0:T(8,128)(2,1)S(1)}, f32[1,384]{1,0:T(1,128)S(1)}) custom-call(f32[1]{0:T(128)S(6)} %copy.16.audio_log_scale.log_scale, f32[1]{0:T(128)S(6)} %copy.17.audio_bias.bias, bf16[400,1024]{1,0:T(8,128)(2,1)S(1)} %collective-permute-done.2.other_video.col_video, ...), custom_call_target="tpu_custom_call" | custom-call | flops 500000000 | bytes 5383168 | tf_op jit(solution)/shard_map/pallas_call | solution.py:281
  49.4 0.1 collective-permute-start.6
  49.4 0.0 collective-permute-done.other_video.row_video
  49.5 0.0 collective-permute-done.1.other_imu.row_imu
  49.5 3.8 %shard_map.134 = (f32[1,384]{1,0:T(1,128)S(1)}, bf16[400,1024]{1,0:T(8,128)(2,1)S(1)}, bf16[384,1024]{1,0:T(8,128)(2,1)S(1)}, bf16[384,384]{1,0:T(8,128)(2,1)S(1)}, bf16[384,384]{1,0:T(8,128)(2,1)S(1)}) custom-call(f32[1]{0:T(128)S(6)} %copy.14.imu_log_scale.log_scale, f32[1]{0:T(128)S(6)} %copy.15.imu_bias.bias, ...), custom_call_target="tpu_custom_call" | custom-call | flops 500000000 | bytes 6556672 | tf_op jit(solution)/shard_map/pallas_call | solution.py:281
  53.3 2.5 %collective-permute-start.7 = (bf16[384,1024]{1,0:T(8,128)(2,1)S(1)}, bf16[384,1024]{1,0:T(8,128)(2,1)S(1)}, u32[]{:S(2)}, u32[]{:S(2)}) collective-permute-start(bf16[384,1024]{1,0:T(8,128)(2,1)S(1)} %get-tuple-element.59), channel_id=1, source_target_pairs={{0,24},{4,28},{8,0},{12,4},{16,8},{20,12},{24,16},{28,20},{1,25},{... | collective-permute-start | bytes 2359304 | tf_op jit(solution)/shard_map/ppermute | solution.py:317
  55.8 0.0 collective-permute-start.5
  55.8 1.9 %shard_map.135 = (f32[384,1024]{1,0:T(8,128)S(1)}, f32[384,1024]{1,0:T(8,128)S(1)}, f32[384,1024]{1,0:T(8,128)S(1)}, f32[1,384]{1,0:T(1,128)S(1)}) custom-call(bf16[384,1024]{1,0:T(8,128)(2,1)S(1)} %collective-permute-done.3.audio.far_audio, bf16[384,384]{1,0:T(8,128)(2,1)S(1)} %get-tuple-element.43.own_weights.far_weights, ...), custom_call_target="tpu_custom_call" | custom-call | flops 10000000 | bytes 18287616 | tf_op jit(solution)/shard_map/pallas_call | solution.py:281
  57.6 8.9 %collective-permute-done.8.got = bf16[384,1024]{1,0:T(8,128)(2,1)S(1)} collective-permute-done((bf16[384,1024]{1,0:T(8,128)(2,1)S(1)}, bf16[384,1024]{1,0:T(8,128)(2,1)S(1)}, u32[]{:S(2)}, u32[]{:S(2)}) %collective-permute-start.8) | collective-permute-done | bytes 786464 | tf_op jit(solution)/shard_map/ppermute | solution.py:317
  66.5 1.2 %shard_map.136 = (f32[384,1024]{1,0:T(8,128)}, f32[1,384]{1,0:T(1,128)S(1)}) custom-call(bf16[384,1024]{1,0:T(8,128)(2,1)S(1)} %collective-permute-done.8.got, f32[384,1024]{1,0:T(8,128)S(1)} %get-tuple-element.62.grad_in, f32[1,384]{1,0:T(1,128)S(1)} %get-tuple-element.63.loss_in), custom_call_target="tpu_custom_call" | custom-call | flops 5000000000 | tf_op jit(solution)/shard_map/pallas_call | solution.py:258
  67.8 6.0 %collective-permute-done.7.got = bf16[384,1024]{1,0:T(8,128)(2,1)S(1)} collective-permute-done((bf16[384,1024]{1,0:T(8,128)(2,1)S(1)}, bf16[384,1024]{1,0:T(8,128)(2,1)S(1)}, u32[]{:S(2)}, u32[]{:S(2)}) %collective-permute-start.7) | collective-permute-done | bytes 786464 | tf_op jit(solution)/shard_map/ppermute | solution.py:317
  73.8 1.2 %shard_map.137 = (f32[384,1024]{1,0:T(8,128)}, f32[1,384]{1,0:T(1,128)S(1)}) custom-call(bf16[384,1024]{1,0:T(8,128)(2,1)S(1)} %collective-permute-done.7.got, f32[384,1024]{1,0:T(8,128)S(1)} %get-tuple-element.60.grad_in, f32[1,384]{1,0:T(1,128)S(1)} %get-tuple-element.64.loss_in), custom_call_target="tpu_custom_call" | custom-call | flops 10000000 | tf_op jit(solution)/shard_map/pallas_call | solution.py:258
  75.0 7.1 %collective-permute-done.6.got_video = bf16[400,1024]{1,0:T(8,128)(2,1)S(1)} collective-permute-done((bf16[400,1024]{1,0:T(8,128)(2,1)S(1)}, bf16[400,1024]{1,0:T(8,128)(2,1)S(1)}, u32[]{:S(2)}, u32[]{:S(2)}) %collective-permute-start.6) | collective-permute-done | bytes 819232 | tf_op jit(solution)/shard_map/ppermute | solution.py:314
  82.1 0.1 shard_map.138
  82.2 0.0 collective-permute-done.5.got_video
  82.3 1.2 %shard_map.139 = (f32[384,1024]{1,0:T(8,128)}, f32[384]{0:T(512)}) custom-call(bf16[400,1024]{1,0:T(8,128)(2,1)S(1)} %collective-permute-done.5.got_video, f32[384,1024]{1,0:T(8,128)S(1)} %get-tuple-element.66.video_in, f32[1,384]{1,0:T(1,128)S(1)} %get-tuple-element.67.loss_in), custom_call_target="tpu_custom_call" | custom-call | flops 500000000 | tf_op jit(solution)/shard_map/pallas_call | solution.py:258
Async XLA Ops:
  0.6 9.2 %copy-start = (bf16[384,1024]{1,0:T(8,128)(2,1)S(1)}, bf16[384,1024]{1,0:T(8,128)(2,1)}, u32[]{:S(2)}) copy-start(bf16[384,1024]{1,0:T(8,128)(2,1)} %audio.3) | copy-start | bytes 2359300
  0.6 9.2 %copy-start.1 = (s32[384]{0:T(512)S(1)}, s32[384]{0:T(512)}, u32[]{:S(2)}) copy-start(s32[384]{0:T(512)} %audio_ids.3) | copy-start | bytes 4612
  0.7 40.6 %collective-permute-start.3 = (bf16[384,1024]{1,0:T(8,128)(2,1)}, bf16[384,1024]{1,0:T(8,128)(2,1)S(1)}, u32[]{:S(2)}, u32[]{:S(2)}) collective-permute-start(bf16[384,1024]{1,0:T(8,128)(2,1)} %audio.3), channel_id=1, source_target_pairs={{3,0},{2,1},{1,2},{0,3},{7,4},{6,5},{5,6},{4,7},{11,8},{10,9},{9,1... | collective-permute-start | bytes 2359304 | tf_op jit(solution)/shard_map/ppermute | solution.py:311
  7.2 35.0 %collective-permute-start.2 = (bf16[400,1024]{1,0:T(8,128)(2,1)S(1)}, bf16[400,1024]{1,0:T(8,128)(2,1)S(1)}, u32[]{:S(2)}, u32[]{:S(2)}) collective-permute-start(bf16[400,1024]{1,0:T(8,128)(2,1)S(1)} %get-tuple-element.38.video), channel_id=1, source_target_pairs={{1,0},{0,1},{3,2},{2,3},{5,4},{4,5},{7,6},{6,7},{9,8},{8,9},{11,10... | collective-permute-start | bytes 2457608 | tf_op jit(solution)/shard_map/ppermute | solution.py:308
  13.8 35.7 %collective-permute-start = (bf16[400,1024]{1,0:T(8,128)(2,1)S(1)}, bf16[400,1024]{1,0:T(8,128)(2,1)S(1)}, u32[]{:S(2)}, u32[]{:S(2)}) collective-permute-start(bf16[400,1024]{1,0:T(8,128)(2,1)S(1)} %get-tuple-element.40), channel_id=1, source_target_pairs={{4,0},{8,4},{12,8},{16,12},{20,16},{24,20},{28,24},{0,28},{5,1},{9... | collective-permute-start | bytes 2457608 | tf_op jit(solution)/shard_map/ppermute | solution.py:308
  15.4 34.0 %collective-permute-start.1 = (bf16[400,1024]{1,0:T(8,128)(2,1)S(1)}, bf16[400,1024]{1,0:T(8,128)(2,1)S(1)}, u32[]{:S(2)}, u32[]{:S(2)}) collective-permute-start(bf16[400,1024]{1,0:T(8,128)(2,1)S(1)} %get-tuple-element.41), channel_id=1, source_target_pairs={{24,0},{28,4},{0,8},{4,12},{8,16},{12,20},{16,24},{20,28},{25,1},{... | collective-permute-start | bytes 2457608 | tf_op jit(solution)/shard_map/ppermute | solution.py:311
  15.4 25.8 %collective-permute-start.4 = (s32[384]{0:T(512)S(1)}, s32[384]{0:T(512)S(1)}, u32[]{:S(2)}, u32[]{:S(2)}) collective-permute-start(s32[384]{0:T(512)S(1)} %copy-done.1), channel_id=1, source_target_pairs={{3,0},{2,1},{1,2},{0,3},{7,4},{6,5},{5,6},{4,7},{11,8},{10,9},{9,1... | collective-permute-start | bytes 4616 | tf_op jit(solution)/shard_map/ppermute | solution.py:311
  44.2 22.4 %collective-permute-start.8 = (bf16[384,1024]{1,0:T(8,128)(2,1)S(1)}, bf16[384,1024]{1,0:T(8,128)(2,1)S(1)}, u32[]{:S(2)}, u32[]{:S(2)}) collective-permute-start(bf16[384,1024]{1,0:T(8,128)(2,1)S(1)} %get-tuple-element.61), channel_id=1, source_target_pairs={{0,3},{1,2},{2,1},{3,0},{4,7},{5,6},{6,5},{7,4},{8,11},{9,10},{10,... | collective-permute-start | bytes 2359304 | tf_op jit(solution)/shard_map/ppermute | solution.py:317
  49.4 32.7 %collective-permute-start.6 = (bf16[400,1024]{1,0:T(8,128)(2,1)S(1)}, bf16[400,1024]{1,0:T(8,128)(2,1)S(1)}, u32[]{:S(2)}, u32[]{:S(2)}) collective-permute-start(bf16[400,1024]{1,0:T(8,128)(2,1)S(1)} %get-tuple-element.50), channel_id=1, source_target_pairs={{0,1},{1,0},{2,3},{3,2},{4,5},{5,4},{6,7},{7,6},{8,9},{9,8},{10,11... | collective-permute-start | bytes 2457608 | tf_op jit(solution)/shard_map/ppermute | solution.py:314
  53.3 20.5 %collective-permute-start.7 = (bf16[384,1024]{1,0:T(8,128)(2,1)S(1)}, bf16[384,1024]{1,0:T(8,128)(2,1)S(1)}, u32[]{:S(2)}, u32[]{:S(2)}) collective-permute-start(bf16[384,1024]{1,0:T(8,128)(2,1)S(1)} %get-tuple-element.59), channel_id=1, source_target_pairs={{0,24},{4,28},{8,0},{12,4},{16,8},{20,12},{24,16},{28,20},{1,25},{... | collective-permute-start | bytes 2359304 | tf_op jit(solution)/shard_map/ppermute | solution.py:317
  55.8 26.5 %collective-permute-start.5 = (bf16[400,1024]{1,0:T(8,128)(2,1)S(1)}, bf16[400,1024]{1,0:T(8,128)(2,1)S(1)}, u32[]{:S(2)}, u32[]{:S(2)}) collective-permute-start(bf16[400,1024]{1,0:T(8,128)(2,1)S(1)} %get-tuple-element.49), channel_id=1, source_target_pairs={{0,4},{4,8},{8,12},{12,16},{16,20},{20,24},{24,28},{28,0},{1,5},{5... | collective-permute-start | bytes 2457608 | tf_op jit(solution)/shard_map/ppermute | solution.py:314
